TPU v7x, 256 devices: a whole 4x4x8 slice. The times are simulated.
256 devices in a mesh: store: 64 (over x, z_lo, y, core), tensor: 4 (over z_hi).
Axes of the slice: x: 4, y: 4, z: 8 (z_hi: 4, z_lo: 2; z = z_hi * 2 + z_lo), core: 2. Of those that a mesh axis runs over, the one named last changes fastest.
Arguments:
- test_inputs: bfloat16 [128, 512, 5120], P('store', None, 'tensor'), may hold values from -6 to 6
- test_cotangents: bfloat16 [128, 512, 5120], P('store', 'tensor'), may hold values from -6 to 6
- train_inputs: bfloat16 [64, 512, 5120], P('store', None, 'tensor'), may hold values from -6 to 6
- train_cotangents: bfloat16 [64, 512, 5120], P('store', 'tensor'), may hold values from -6 to 6
- test_lengths: int32 [128], P('store'), may hold values from 64 to 512, as said below
- train_lengths: int32 [64], P('store'), may hold values from 64 to 512, as said below
- in_projection: bfloat16 [64, 5120], P(None, 'tensor'), may hold values from -0.078125 to 0.078125
- out_projection: bfloat16 [64, 5120], replicated, may hold values from -0.078125 to 0.078125
- in_inverse: float32 [64, 64], replicated, as said below
- out_inverse: float32 [64, 64], replicated, as said below
- store: bfloat16 [131072, 4096], P(('store', 'tensor')), may hold values from -0.59765625 to 0.59765625
Outputs:
- store_scores: float32 [128, 131072], P(None, ('store', 'tensor'))
- fresh_scores: float32 [128, 64], P(None, 'store')
Inputs may be any that keep to these rules, and one draw needn't show every extreme that they name: `test_lengths`: positions at or past a pair's length are padding. `train_lengths`: positions at or past a pair's length are padding. `in_inverse`: symmetric positive definite. `out_inverse`: symmetric positive definite.
All inputs are finite; a program needn't handle non-finite values.
Results may differ from a plain program's by a relative error of at most 0.024.
Values may be sent and summed in bfloat16 or wider, within the bound.
A program may use at most 128 MiB of HBM per device.

v0:
```python
import jax
import jax.numpy as jnp
from jax import lax
from jax.sharding import PartitionSpec as P


def local_terms(inputs, cotangents, lengths, in_projection, out_projection, positions):
    projected_in = jnp.einsum(
        "nld,rd->nrl", inputs, in_projection, preferred_element_type=jnp.float32
    )
    projected_out = jnp.einsum(
        "nld,rd->nrl", cotangents, out_projection, preferred_element_type=jnp.float32
    )
    kept_mask = (positions[None, :] < lengths[:, None]).astype(jnp.float32)
    scaled_mask = kept_mask / lengths.astype(jnp.float32)[:, None]
    return (projected_in, projected_out * scaled_mask[:, None, :])


def body(
    test_inputs,
    test_cotangents,
    train_inputs,
    train_cotangents,
    test_lengths,
    train_lengths,
    in_projection,
    out_projection,
    in_inverse,
    out_inverse,
    store,
):
    quarter = test_cotangents.shape[1]
    positions = lax.axis_index("tensor") * quarter + jnp.arange(quarter, dtype=jnp.int32)
    test_in, test_out = local_terms(
        test_inputs, test_cotangents, test_lengths, in_projection, out_projection, positions
    )
    train_in, train_out = local_terms(
        train_inputs, train_cotangents, train_lengths, in_projection, out_projection, positions
    )
    full_test_in, full_train_in = lax.psum((test_in, train_in), "tensor")
    full_test_out, full_train_out = (
        lax.all_gather(test_out, "tensor", axis=2, tiled=True),
        lax.all_gather(train_out, "tensor", axis=2, tiled=True),
    )
    test_factors = jnp.einsum("nol,nil->noi", full_test_out, full_test_in)
    train_factors = jnp.einsum("nol,nil->noi", full_train_out, full_train_in)
    highest = lax.Precision.HIGHEST
    conditioned = jnp.einsum("ab,nbc->nac", out_inverse, test_factors, precision=highest)
    conditioned = jnp.einsum("nac,cd->nad", conditioned, in_inverse, precision=highest)
    flat_size = conditioned.shape[1] * conditioned.shape[2]
    conditioned = conditioned.astype(jnp.bfloat16).reshape(conditioned.shape[0], flat_size)
    train_flat = train_factors.astype(jnp.bfloat16).reshape(train_factors.shape[0], flat_size)
    block_rows = lax.all_gather(conditioned, "store", axis=0, tiled=True)
    against_store = lax.dot_general(
        block_rows, store, (((1,), (1,)), ((), ())), preferred_element_type=jnp.float32
    )
    against_fresh = lax.dot_general(
        block_rows, train_flat, (((1,), (1,)), ((), ())), preferred_element_type=jnp.float32
    )
    scored = jnp.concatenate([against_store, against_fresh], axis=1)
    stored_count = store.shape[0]
    return (scored[:, :stored_count], scored[:, stored_count:])


def solution(mesh):
    return jax.shard_map(
        body,
        mesh=mesh,
        in_specs=(
            P("store", None, "tensor"),
            P("store", "tensor", None),
            P("store", None, "tensor"),
            P("store", "tensor", None),
            P("store"),
            P("store"),
            P(None, "tensor"),
            P(),
            P(),
            P(),
            P(("store", "tensor"), None),
        ),
        out_specs=(P(None, ("store", "tensor")), P(None, "store")),
        check_vma=False,
    )
```

profile of v0, /device:TPU:1, one launch (start us, length us, event | category | flops | bytes accessed | tf_op | source)
XLA Modules:
  0.0 178.9 jit_solution(7658020364240844482)
XLA Ops:
  7.2 0.0 copy-start
  7.2 0.0 copy-start.3
  7.2 0.0 all-gather.4.cloned.1.call-start
  7.2 0.0 copy-start.2
  7.3 0.8 convert_element_type.25
  8.1 0.8 fusion.17
  8.9 2.9 %fusion.7 = f32[64,2,128]{2,0,1:T(8,128)S(1)} fusion(bf16[2,128,5120]{2,1,0:T(8,128)(2,1)} %param.12, bf16[64,5120]{1,0:T(8,128)(2,1)} %param.18), kind=kOutput, calls=%fused_computation.9 | convolution fusion | flops 167772160 | bytes 3342336 | tf_op jit(solution)/shard_map/nld,rd->nrl/dot_general | solution.py:11
  11.8 0.1 fusion.14
  11.8 14.1 %all_gather.9 = bf16[2,64,512]{2,0,1:T(2,128)(2,1)} all-gather(bf16[2,64,128]{2,0,1:T(2,128)(2,1)S(1)} %fusion.14), channel_id=1, replica_groups=mesh['store'=64,'tensor'=4] {'tensor'}, dimensions={2}, use_global_device_ids=true | all-gather | bytes 163840 | tf_op jit(solution)/shard_map/all_gather | solution.py:42
  25.9 0.0 copy-done.3
  25.9 0.0 copy-done.2
  25.9 1.2 fusion
  27.1 0.0 copy-done
  27.1 0.0 copy-start.1
  27.1 0.9 fusion.12
  28.0 0.2 copy.25
  28.2 21.6 %all-reduce.2 = (bf16[2,64,512]{2,0,1:T(2,128)(2,1)}, bf16[64,512]{1,0:T(8,128)(2,1)}) all-reduce(f32[2,64,512]{2,0,1:T(2,128)S(1)} %bitcast.45, f32[64,512]{1,0:T(8,128)} %fusion), channel_id=1, replica_groups=mesh['store'=64,'tensor'=4] {'tensor'}, use_global_device_ids=true, to_apply=%region_0.0 | all-reduce | flops 98304 | bytes 589824 | tf_op jit(solution)/shard_map/psum | solution.py:40
  49.8 0.0 copy-start.4
  49.8 1.1 fusion.9
  51.0 1.0 convolution_bitcast_fusion
  51.9 1.0 convolution_convert_fusion
  52.9 0.7 reshape.105
  53.6 0.0 all-gather.4.cloned.1.call-update
  54.3 0.0 copy-done.1
  54.3 1.9 %fusion.4 = bf16[64,128]{1,0:T(8,128)(2,1)S(1)} fusion(bf16[64,5120]{1,0:T(8,128)(2,1)S(1)} %copy-done.1, bf16[1,128,5120]{2,1,0:T(8,128)(2,1)} %param.14, f32[128]{0:T(128)S(1)} %compare_select_fusion), kind=kOutput, calls=%fused_computation.6 | convolution fusion | flops 83902464 | bytes 1982976 | tf_op jit(solution)/shard_map/nld,rd->nrl/dot_general | solution.py:11
  56.2 10.7 %all-gather = bf16[64,512]{1,0:T(8,128)(2,1)S(1)} all-gather(bf16[64,128]{1,0:T(8,128)(2,1)S(1)} %fusion.4), channel_id=2, replica_groups=mesh['store'=64,'tensor'=4] {'tensor'}, dimensions={1}, use_global_device_ids=true | all-gather | bytes 81920 | tf_op jit(solution)/shard_map/all_gather | solution.py:43
  66.9 0.0 copy-done.4
  66.9 0.1 fusion.19
  67.1 0.1 reshape.112
  67.2 95.8 %all-gather.4.cloned.1.call-done = bf16[64,2,4096]{2,1,0:T(2,128)(2,1)} async-done(((bf16[1,2,4096]{2,1,0:T(2,128)(2,1)}), bf16[64,2,4096]{2,1,0:T(2,128)(2,1)}) %all-gather.4.cloned.1.call-update) | async-done | bytes 1048592 | tf_op jit(solution)/shard_map/all_gather | solution.py:53
  162.9 2.3 %reshape.106 = bf16[128,4096]{1,0:T(8,128)(2,1)} reshape(bf16[64,2,4096]{2,1,0:T(2,128)(2,1)} %all-gather.4.cloned.1.call-done) | data formatting | bytes 2097152
  165.2 2.1 %convolution_bitcast_fusion.1 = f32[128,1]{0,1:T(1,128)} fusion(bf16[128,4096]{1,0:T(8,128)(2,1)} %reshape.106, bf16[4096,1]{0,1:T(2,128)(2,1)S(1)} %reshape.112), kind=kOutput, calls=%fused_computation.8 | convolution fusion | flops 1048576 | bytes 1057280 | tf_op jit(solution)/shard_map/dot_general | solution.py:57
  167.3 4.7 %fusion.18 = f32[128,512]{1,0:T(8,128)} fusion(bf16[128,4096]{1,0:T(8,128)(2,1)} %reshape.106, bf16[512,4096]{1,0:T(8,128)(2,1)} %param.21), kind=kOutput, calls=%fused_computation.25 | convolution fusion | flops 536870912 | bytes 5505024 | tf_op jit(solution)/shard_map/dot_general | solution.py:54
  (2 shorter events, 0.0 us)
Async XLA Ops:
  7.2 19.9 %copy-start = (bf16[2,512,1280]{2,1,0:T(8,128)(2,1)S(1)}, bf16[2,512,1280]{2,1,0:T(8,128)(2,1)}, u32[]{:S(2)}) copy-start(bf16[2,512,1280]{2,1,0:T(8,128)(2,1)} %param.11) | copy-start | bytes 7864324
  7.2 18.7 %copy-start.3 = (bf16[64,1280]{1,0:T(8,128)(2,1)S(1)}, bf16[64,1280]{1,0:T(8,128)(2,1)}, u32[]{:S(2)}) copy-start(bf16[64,1280]{1,0:T(8,128)(2,1)} %param.17) | copy-start | bytes 491524
  7.2 155.8 %all-gather.4.cloned.1.call-start = ((), (), s32[]{:S(2)}) async-start(), calls=%async_computation | async-start | bytes 1064960 | tf_op jit(solution)/shard_map/all_gather | solution.py:53
  7.2 18.7 %copy-start.2 = (bf16[1,512,1280]{2,1,0:T(8,128)(2,1)S(1)}, bf16[1,512,1280]{2,1,0:T(8,128)(2,1)}, u32[]{:S(2)}) copy-start(bf16[1,512,1280]{2,1,0:T(8,128)(2,1)} %param.13) | copy-start | bytes 3932164
  27.1 27.2 %copy-start.1 = (bf16[64,5120]{1,0:T(8,128)(2,1)S(1)}, bf16[64,5120]{1,0:T(8,128)(2,1)}, u32[]{:S(2)}) copy-start(bf16[64,5120]{1,0:T(8,128)(2,1)} %param.18) | copy-start | bytes 1966084
  49.8 17.1 %copy-start.4 = (bf16[64,512]{1,0:T(8,128)(2,1)S(1)}, bf16[64,512]{1,0:T(8,128)(2,1)}, u32[]{:S(2)}) copy-start(bf16[64,512]{1,0:T(8,128)(2,1)} %get-tuple-element.3) | copy-start | bytes 196612
Sparse Core Ops, SparseCore 0:
  53.8 109.1 all-gather.3
where the time goes:
time: 179 us
  waiting for transfers between devices  95.8 us (54%)
  blocking collectives  46.4 us (26%)
  matrix products  16.9 us (9%)
  between operations  14.8 us (8%)
  local copies, waits for them, and re-layouts  3.3 us (2%)
    all_gather x1, waiting for transfers between devices, body(): block_rows = lax.all_gather(conditioned, 'store', axis=0, tiled=True)  95.8 us
    psum x1, blocking collectives, body(): full_test_in, full_train_in = lax.psum((test_in, train_in), 'tensor')  21.6 us
    all_gather x1, blocking collectives, body(): lax.all_gather(test_out, 'tensor', axis=2, tiled=True)  14.1 us
    all_gather x1, blocking collectives, body(): lax.all_gather(train_out, 'tensor', axis=2, tiled=True)  10.7 us
    dot_general x2, matrix products, local_terms(): jnp.einsum('nld,rd->nrl', cotangents, out_projection, preferred_element_t...  4.76 us
    dot_general x1, matrix products, body(): lax.dot_general(block_rows, store, (((1,), (1,)), ((), ())), preferred_el...  4.75 us
  transfers between devices with their start and end apart: 1, of which 1 were waited for; matrix products, arithmetic and copies ran while one was open for 1% of the time, Pallas kernels for 0%

commit v1 on v0

v1 whole, which is shorter than its diff:
```python
import jax
import jax.numpy as jnp
from jax import lax
from jax.experimental import pallas as pl
from jax.experimental.pallas import tpu as pltpu
from jax.sharding import PartitionSpec as P

MESH = pl.DeviceIdType.MESH
F32 = jnp.float32
BF16 = jnp.bfloat16
HIGHEST = lax.Precision.HIGHEST
NT = (((1,), (1,)), ((), ()))

NX, NZL, NY, NC, NT4 = 4, 2, 4, 2, 4
R = 64
QUARTER = 128
LEN = 512
HALF = 2048
CHUNKS = 2
CHUNK = HALF // CHUNKS


def remote(src, dst, send_sem, recv_sem, device):
    return pltpu.make_async_remote_copy(
        src_ref=src,
        dst_ref=dst,
        send_sem=send_sem,
        recv_sem=recv_sem,
        device_id=device,
        device_id_type=MESH,
    )


def mod4(value):
    return lax.rem(value + 4, 4)


def kernel(
    tin_ref,
    tcot_ref,
    rin_ref,
    rcot_ref,
    tlen_ref,
    rlen_ref,
    win_ref,
    wout_ref,
    iinv_ref,
    oinv_ref,
    store_ref,
    scores_ref,
    fresh_ref,
    tin,
    tcot,
    rin,
    rcot,
    win,
    wout,
    iinv,
    oinv,
    store,
    po,
    part_send,
    part_recv,
    mine,
    gath,
    swap,
    full,
    acc,
    accf,
    rpo,
    rscr,
    rpart_send,
    rpart_recv,
    trow,
    trowb,
    load_sem,
    po_send,
    po_recv,
    rs_send,
    rs_recv,
    col_send,
    col_recv,
    s4_send,
    s4_recv,
    s5_send,
    s5_recv,
    fw_send,
    fw_recv,
    rpo_send,
    rpo_recv,
    rrs_send,
    rrs_recv,
):
    me = lax.axis_index("store")
    t = lax.axis_index("tensor")
    c = lax.rem(me, 2)
    y = lax.rem(lax.div(me, 2), 4)
    zl = lax.rem(lax.div(me, 8), 2)
    x = lax.div(me, 16)

    def index(xx, zz, yy, cc):
        return ((xx * 2 + zz) * 4 + yy) * 2 + cc

    early = [
        pltpu.make_async_copy(wout_ref, wout, load_sem.at[0]),
        pltpu.make_async_copy(tcot_ref, tcot, load_sem.at[1]),
        pltpu.make_async_copy(oinv_ref, oinv, load_sem.at[2]),
        pltpu.make_async_copy(iinv_ref, iinv, load_sem.at[3]),
        pltpu.make_async_copy(win_ref, win, load_sem.at[4]),
        pltpu.make_async_copy(tin_ref, tin, load_sem.at[5]),
    ]
    late = [
        pltpu.make_async_copy(rcot_ref.at[0], rcot, load_sem.at[6]),
        pltpu.make_async_copy(rin_ref.at[0], rin, load_sem.at[7]),
        pltpu.make_async_copy(store_ref, store, load_sem.at[8]),
    ]
    for copy in early:
        copy.start()

    barrier = pltpu.get_barrier_semaphore()
    partners = []
    for dt in range(4):
        for dz in range(2):
            for dc in range(2):
                if dt or dz or dc:
                    partners.append(
                        (index(x, lax.rem(zl + dz, 2), y, lax.rem(c + dc, 2)), mod4(t + dt))
                    )
    for k in range(1, 4):
        partners.append((index(mod4(x + k), zl, y, c), t))
        partners.append((index(x, zl, mod4(y + k), c), t))
    for partner in partners:
        pl.semaphore_signal(barrier, inc=1, device_id=partner, device_id_type=MESH)

    lane = lax.broadcasted_iota(jnp.int32, (1, QUARTER), 1) + t * QUARTER

    def scale_of(length):
        lengths = jnp.full((1, QUARTER), length, jnp.int32)
        kept = jnp.where(lane < lengths, 1.0, 0.0).astype(F32)
        return kept / lengths.astype(F32)

    early[0].wait()
    early[1].wait()
    pout = lax.dot_general(
        wout[...], tcot[...].reshape(2 * QUARTER, 5120), NT, preferred_element_type=F32
    )
    scale = jnp.concatenate([scale_of(tlen_ref[0]), scale_of(tlen_ref[1])], axis=1)
    pout = pout * scale
    early[2].wait()
    left = jnp.concatenate(
        [oinv[pl.ds(0, 32, stride=2), :], oinv[pl.ds(1, 32, stride=2), :]], axis=0
    )
    pout = jnp.dot(left, pout, precision=HIGHEST, preferred_element_type=F32)
    po[t] = pout.astype(BF16)

    pl.semaphore_wait(barrier, len(partners))
    po_copies = []
    for k in range(1, 4):
        copy = remote(
            po.at[t], po.at[t], po_send.at[k - 1], po_recv.at[k - 1], (me, mod4(t + k))
        )
        copy.start()
        po_copies.append(copy)
    for copy in late:
        copy.start()

    early[3].wait()
    early[4].wait()
    early[5].wait()
    pin = lax.dot_general(
        win[...], tin[...].reshape(2 * LEN, 1280), NT, preferred_element_type=F32
    )
    pin = jnp.dot(iinv[...], pin, precision=HIGHEST, preferred_element_type=F32)
    pin = pin.astype(BF16)

    late[0].wait()
    rout = lax.dot_general(wout[...], rcot[...], NT, preferred_element_type=F32)
    rout = rout * scale_of(rlen_ref[0])
    rpo[t] = rout.astype(BF16)
    late[1].wait()
    rpin = lax.dot_general(win[...], rin[...], NT, preferred_element_type=F32).astype(BF16)

    for k in range(1, 4):
        slot = mod4(t - k)
        remote(
            po.at[slot], po.at[slot], po_send.at[k - 1], po_recv.at[k - 1], (me, slot)
        ).wait_recv()

    for n in range(2):
        outs = jnp.concatenate(
            [po[u, :, n * QUARTER : (n + 1) * QUARTER] for u in range(4)], axis=1
        )
        part = lax.dot_general(
            outs, pin[:, n * LEN : (n + 1) * LEN], NT, preferred_element_type=F32
        )
        packed = jnp.concatenate([part[:32], part[32:]], axis=1)
        for u in range(4):
            part_send[u, n] = packed[8 * u : 8 * u + 8]

    rs_copies = []
    for k in range(1, 4):
        to = mod4(t + k)
        copy = remote(
            part_send.at[to], part_recv.at[k - 1], rs_send.at[k - 1], rs_recv.at[k - 1], (me, to)
        )
        copy.start()
        rs_copies.append(copy)
    for copy in rs_copies:
        copy.wait_recv()
    total = part_send[t] + part_recv[0] + part_recv[1] + part_recv[2]
    mine[...] = total.reshape(16, 128).astype(BF16)

    h = lax.div(t, 2)
    a_h = x * (1 - h) + y * h
    slot = (zl * 2 + c) * 2 + lax.rem(t, 2)
    col_copies = []
    for dt in range(4):
        for dz in range(2):
            i = dt * 2 + dz
            if i:
                copy = remote(
                    mine,
                    gath.at[a_h, slot],
                    col_send.at[i],
                    col_recv.at[slot],
                    (index(x, lax.rem(zl + dz, 2), y, h), mod4(t + dt)),
                )
                copy.start()
                col_copies.append(copy)

    own_copy = pltpu.make_async_copy(mine, gath.at[a_h, slot], col_recv.at[slot])
    sib_copy = remote(
        mine, gath.at[a_h, slot], col_send.at[0], col_recv.at[slot], (index(x, zl, y, h), t)
    )

    @pl.when(h == c)
    def _():
        own_copy.start()

    @pl.when(h != c)
    def _():
        sib_copy.start()

    rpo_copies = []
    for k in range(1, 4):
        copy = remote(
            rpo.at[t], rpo.at[t], rpo_send.at[k - 1], rpo_recv.at[k - 1], (me, mod4(t + k))
        )
        copy.start()
        rpo_copies.append(copy)

    a = x * (1 - c) + y * c
    for i in range(8):
        pltpu.make_async_copy(mine, gath.at[a, i], col_recv.at[i]).wait()

    s4_copies = []
    for k in range(1, 4):
        to = index(mod4(x + k * (1 - c)), zl, mod4(y + k * c), c)
        copy = remote(gath.at[a], gath.at[a], s4_send.at[k - 1], s4_recv.at[k - 1], (to, t))
        copy.start()
        s4_copies.append(copy)

    for k in range(1, 4):
        from_t = mod4(t - k)
        remote(
            rpo.at[from_t], rpo.at[from_t], rpo_send.at[k - 1], rpo_recv.at[k - 1], (me, from_t)
        ).wait_recv()
    routs = jnp.concatenate([rpo[u] for u in range(4)], axis=1)
    rscr[...] = lax.dot_general(routs, rpin, NT, preferred_element_type=F32)
    rpart_send[...] = jnp.concatenate(
        [rscr[pl.ds(0, 32, stride=2), :], rscr[pl.ds(1, 32, stride=2), :]], axis=1
    )
    rrs_copies = []
    for k in range(1, 4):
        copy = remote(
            rpart_send,
            rpart_recv.at[k - 1],
            rrs_send.at[k - 1],
            rrs_recv.at[k - 1],
            (me, mod4(t + k)),
        )
        copy.start()
        rrs_copies.append(copy)

    for k in range(1, 4):
        slot_in = mod4(a - k)
        remote(
            gath.at[slot_in], gath.at[slot_in], s4_send.at[k - 1], s4_recv.at[k - 1], (me, t)
        ).wait_recv()

    q = y * (1 - c) + x * c
    for pair in range(2):
        for j in range(2):
            blocks = []
            for aa in (2 * pair, 2 * pair + 1):
                rows = [gath[aa, s * 2 + j].astype(F32).reshape(2, 8, 128) for s in range(4)]
                blocks.append(jnp.swapaxes(jnp.concatenate(rows, axis=0), 0, 1))
            both = jnp.concatenate(blocks, axis=1).astype(BF16)
            for e in range(8):
                full[c, j, q, pair * 16 : pair * 16 + 16, e * 128 : (e + 1) * 128] = both[e]

    sib = index(x, zl, y, 1 - c)
    s5_copies, fw_copies = [], []

    def forward(j, i, at):
        copy = remote(
            full.at[c, j, at], full.at[c, j, at], fw_send.at[j, i], fw_recv.at[j, i], (sib, t)
        )
        copy.start()
        fw_copies.append(copy)

    for j in range(CHUNKS):
        for k in range(1, 4):
            to = index(mod4(x + k * c), zl, mod4(y + k * (1 - c)), c)
            copy = remote(
                full.at[c, j, q],
                full.at[c, j, q],
                s5_send.at[j, k - 1],
                s5_recv.at[j, k - 1],
                (to, t),
            )
            copy.start()
            s5_copies.append(copy)
    for j in range(CHUNKS):
        forward(j, 0, q)

    for copy in rrs_copies:
        copy.wait_recv()
    rtotal = rpart_send[...] + rpart_recv[0] + rpart_recv[1] + rpart_recv[2]
    trow[...] = jnp.zeros_like(trow)
    for e in range(32):
        trow[0:1, e * 128 : (e + 1) * 128] = rtotal[e : e + 1]
    trowb[...] = trow[...].astype(BF16)

    late[2].wait()

    def scores_of(hh, j):
        lhs = full[hh, j].reshape(4 * 32, CHUNK)
        columns = pl.ds(pl.multiple_of(hh * HALF + j * CHUNK, 128), CHUNK)
        value = lax.dot_general(lhs, store[:, columns], NT, preferred_element_type=F32)
        valuef = lax.dot_general(lhs, trowb[:, columns], NT, preferred_element_type=F32)
        if j == 0:
            acc[hh] = value
            accf[hh] = valuef
        else:
            acc[hh] += value
            accf[hh] += valuef

    for j in range(CHUNKS):
        for k in range(1, 4):
            at = mod4(q - k)
            remote(
                full.at[c, j, at], full.at[c, j, at], s5_send.at[j, k - 1], s5_recv.at[j, k - 1], (me, t)
            ).wait_recv()
            forward(j, k, at)
        scores_of(c, j)
    for j in range(CHUNKS):
        for i in range(4):
            at = mod4(a - i)
            remote(
                full.at[1 - c, j, at], full.at[1 - c, j, at], fw_send.at[j, i], fw_recv.at[j, i], (sib, t)
            ).wait_recv()
        scores_of(1 - c, j)

    for xx in range(4):
        for yp in range(2):
            block, blockf = [], []
            for yy in (2 * yp, 2 * yp + 1):
                i0, i1 = (yy * 4 + xx) * 8, (xx * 4 + yy) * 8
                block.append(acc[0, i0 : i0 + 8] + acc[1, i1 : i1 + 8])
                blockf.append(accf[0, i0 : i0 + 8] + accf[1, i1 : i1 + 8])
            for zz in range(2):
                row = xx * 32 + zz * 16 + yp * 8
                cut = slice(zz * 4, zz * 4 + 4)
                scores_ref[row : row + 8, :] = jnp.concatenate([b[cut] for b in block], axis=0)
                fresh_ref[row : row + 8, :] = jnp.concatenate(
                    [b[cut, 0:1] for b in blockf], axis=0
                )

    for copy in (
        po_copies + rs_copies + col_copies + rpo_copies + s4_copies + rrs_copies + s5_copies + fw_copies
    ):
        copy.wait_send()

    @pl.when(h != c)
    def _():
        sib_copy.wait_send()


def body(*args):
    dma = pltpu.SemaphoreType.DMA
    anywhere = pl.BlockSpec(memory_space=pl.ANY)
    smem = pl.BlockSpec(memory_space=pltpu.SMEM)
    vmem = pl.BlockSpec(memory_space=pltpu.VMEM)
    return pl.pallas_call(
        kernel,
        out_shape=(
            jax.ShapeDtypeStruct((128, 512), F32),
            jax.ShapeDtypeStruct((128, 1), F32),
        ),
        in_specs=[anywhere] * 4 + [smem] * 2 + [anywhere] * 5,
        out_specs=(vmem, vmem),
        scratch_shapes=[
            pltpu.VMEM((2, LEN, 1280), BF16),
            pltpu.VMEM((2, QUARTER, 5120), BF16),
            pltpu.VMEM((LEN, 1280), BF16),
            pltpu.VMEM((QUARTER, 5120), BF16),
            pltpu.VMEM((R, 1280), BF16),
            pltpu.VMEM((R, 5120), BF16),
            pltpu.VMEM((R, R), F32),
            pltpu.VMEM((R, R), F32),
            pltpu.VMEM((512, 4096), BF16),
            pltpu.VMEM((4, R, 2 * QUARTER), BF16),
            pltpu.VMEM((4, 2, 8, 128), F32),
            pltpu.VMEM((3, 2, 8, 128), F32),
            pltpu.VMEM((16, 128), BF16),
            pltpu.VMEM((4, 8, 16, 128), BF16),
            pltpu.VMEM((8, 128), F32),
            pltpu.VMEM((2, CHUNKS, 4, 32, CHUNK), BF16),
            pltpu.VMEM((2, 128, 512), F32),
            pltpu.VMEM((2, 128, 16), F32),
            pltpu.VMEM((4, R, QUARTER), BF16),
            pltpu.VMEM((R, R), F32),
            pltpu.VMEM((32, 128), F32),
            pltpu.VMEM((3, 32, 128), F32),
            pltpu.VMEM((16, 4096), F32),
            pltpu.VMEM((16, 4096), BF16),
            dma((9,)),
            dma((3,)),
            dma((3,)),
            dma((3,)),
            dma((3,)),
            dma((8,)),
            dma((8,)),
            dma((3,)),
            dma((3,)),
            dma((CHUNKS, 3)),
            dma((CHUNKS, 3)),
            dma((CHUNKS, 4)),
            dma((CHUNKS, 4)),
            dma((3,)),
            dma((3,)),
            dma((3,)),
            dma((3,)),
        ],
        compiler_params=pltpu.CompilerParams(
            collective_id=0, has_side_effects=True, vmem_limit_bytes=48 * 1024 * 1024
        ),
    )(*args)


def solution(mesh):
    return jax.shard_map(
        body,
        mesh=mesh,
        in_specs=(
            P("store", None, "tensor"),
            P("store", "tensor", None),
            P("store", None, "tensor"),
            P("store", "tensor", None),
            P("store"),
            P("store"),
            P(None, "tensor"),
            P(),
            P(),
            P(),
            P(("store", "tensor"), None),
        ),
        out_specs=(P(None, ("store", "tensor")), P(None, "store")),
        check_vma=False,
    )
```

time: 179 us -> 49.6 us (0.28)
  waiting for transfers between devices: 95.8 us -> 0 us
  blocking collectives: 46.4 us -> 0 us
  Pallas kernels: 0 us -> 39.9 us
  matrix products: 16.9 us -> 0 us
  between operations: 14.8 us -> 1.3 us
  local copies, waits for them, and re-layouts: 3.3 us -> 8.08 us
    all_gather x1 -> x0, waiting for transfers between devices: 95.8 us -> none  [body(): block_rows = lax.all_gather(conditioned, 'store', axis=0, tiled=True)]
    pallas_call x0 -> x1, Pallas kernels: none -> 39.9 us  [body(): pl.pallas_call(kernel, out_shape=(jax.ShapeDtypeStruct((128, 512), F32),...]
    all_gather x2 -> x0, blocking collectives: 24.8 us -> none  [the longest x1 14.1 us: body(): lax.all_gather(test_out, 'tensor', axis=2, tiled=True)]
    psum x1 -> x0, blocking collectives: 21.6 us -> none  [body(): full_test_in, full_train_in = lax.psum((test_in, train_in), 'tensor')]
    dot_general x10 -> x0, matrix products: 16.9 us -> none  [the longest x2 4.76 us: local_terms(): jnp.einsum('nld,rd->nrl', cotangents, out_projection, preferred_element_t...]
    unnamed x12 -> x15, local copies, waits for them, and re-layouts: 3.01 us -> 7.5 us
  transfers between devices with their start and end apart: 1 -> 0, of which waited for: 1 -> 0; matrix products, arithmetic and copies ran while one was open for 1% -> 0% of each run, Pallas kernels for 0% -> 0%
where the time goes in v1:
time: 49.6 us; the launch traced here: 49.3 us
  Pallas kernels  39.9 us (80%)
  local copies, waits for them, and re-layouts  8.08 us (16%)
  between operations  1.3 us (3%)
    pallas_call x1, Pallas kernels, body(): pl.pallas_call(kernel, out_shape=(jax.ShapeDtypeStruct((128, 512), F32),...  39.9 us
    unnamed x15, local copies, waits for them, and re-layouts  7.5 us

profile of v1, /device:TPU:1, one launch (start us, length us, event | category | flops | bytes accessed | tf_op | source)
XLA Modules:
  0.0 49.3 jit_solution(13886122383317526087)
XLA Ops:
  1.3 0.0 copy-start
  1.3 1.3 %copy-done = bf16[1,512,1280]{2,1,0:T(8,128)(2,1)S(1)} copy-done((bf16[1,512,1280]{2,1,0:T(8,128)(2,1)S(1)}, bf16[1,512,1280]{2,1,0:T(8,128)(2,1)}, u32[]{:S(2)}) %copy-start) | copy-done | bytes 1310744
  2.6 0.0 copy-start.1
  2.6 1.3 %copy-done.1 = bf16[1,128,5120]{2,1,0:T(8,128)(2,1)S(1)} copy-done((bf16[1,128,5120]{2,1,0:T(8,128)(2,1)S(1)}, bf16[1,128,5120]{2,1,0:T(8,128)(2,1)}, u32[]{:S(2)}) %copy-start.1) | copy-done | bytes 1310744
  3.9 0.0 copy-start.2
  3.9 1.1 %copy-done.2 = bf16[64,5120]{1,0:T(8,128)(2,1)S(1)} copy-done((bf16[64,5120]{1,0:T(8,128)(2,1)S(1)}, bf16[64,5120]{1,0:T(8,128)(2,1)}, u32[]{:S(2)}) %copy-start.2) | copy-done | bytes 655384
  5.0 0.0 copy-start.3
  5.0 0.9 %copy-done.3 = bf16[64,1280]{1,0:T(8,128)(2,1)S(1)} copy-done((bf16[64,1280]{1,0:T(8,128)(2,1)S(1)}, bf16[64,1280]{1,0:T(8,128)(2,1)}, u32[]{:S(2)}) %copy-start.3) | copy-done | bytes 163864
  5.9 0.0 copy-start.4
  5.9 0.8 %copy-done.4 = f32[64,64]{1,0:T(8,128)S(1)} copy-done((f32[64,64]{1,0:T(8,128)S(1)}, f32[64,64]{1,0:T(8,128)}, u32[]{:S(2)}) %copy-start.4) | copy-done | bytes 16408
  6.7 0.0 copy-start.5
  6.7 0.8 %copy-done.5 = f32[64,64]{1,0:T(8,128)S(1)} copy-done((f32[64,64]{1,0:T(8,128)S(1)}, f32[64,64]{1,0:T(8,128)}, u32[]{:S(2)}) %copy-start.5) | copy-done | bytes 16408
  7.4 0.0 copy-start.6
  7.4 0.7 %copy-done.6 = s32[2]{0:T(128)S(1)} copy-done((s32[2]{0:T(128)S(1)}, s32[2]{0:T(128)}, u32[]{:S(2)}) %copy-start.6) | copy-done | bytes 32
  8.1 39.9 %shard_map.122 = (f32[128,512]{1,0:T(8,128)S(1)}, f32[128,1]{1,0:T(8,128)S(1)}) custom-call(bf16[2,512,1280]{2,1,0:T(8,128)(2,1)} %tin_ref.1, bf16[2,128,5120]{2,1,0:T(8,128)(2,1)} %tcot_ref.1, bf16[1,512,1280]{2,1,0:T(8,128)(2,1)S(1)} %copy-done, bf16[1,128,5120]{2,1,0:T(8,128)(2,1)S(1)} %copy-done.1, s32[2]{0:T(128)S(1)} %copy-done.6, ...), custom_call_target="tpu_custom_call" | custom-call | tf_op jit(solution)/shard_map/pallas_call | solution.py:395
  48.0 0.6 %copy.13 = f32[128,1]{0,1:T(1,128)} copy(f32[128,1]{1,0:T(8,128)S(1)} %get-tuple-element.3) | data formatting | bytes 1024 | tf_op jit(solution)/shard_map/pallas_call | solution.py:395
  48.6 0.7 %copy.16 = f32[128,512]{1,0:T(8,128)} copy(f32[128,512]{1,0:T(8,128)S(1)} %get-tuple-element.6) | data formatting | bytes 524288
Async XLA Ops:
  1.3 1.3 %copy-start = (bf16[1,512,1280]{2,1,0:T(8,128)(2,1)S(1)}, bf16[1,512,1280]{2,1,0:T(8,128)(2,1)}, u32[]{:S(2)}) copy-start(bf16[1,512,1280]{2,1,0:T(8,128)(2,1)} %rin_ref.1) | copy-start | bytes 3932164
  2.6 1.3 %copy-start.1 = (bf16[1,128,5120]{2,1,0:T(8,128)(2,1)S(1)}, bf16[1,128,5120]{2,1,0:T(8,128)(2,1)}, u32[]{:S(2)}) copy-start(bf16[1,128,5120]{2,1,0:T(8,128)(2,1)} %rcot_ref.1) | copy-start | bytes 3932164
  3.9 1.1 %copy-start.2 = (bf16[64,5120]{1,0:T(8,128)(2,1)S(1)}, bf16[64,5120]{1,0:T(8,128)(2,1)}, u32[]{:S(2)}) copy-start(bf16[64,5120]{1,0:T(8,128)(2,1)} %wout_ref.1) | copy-start | bytes 1966084
  5.0 0.9 %copy-start.3 = (bf16[64,1280]{1,0:T(8,128)(2,1)S(1)}, bf16[64,1280]{1,0:T(8,128)(2,1)}, u32[]{:S(2)}) copy-start(bf16[64,1280]{1,0:T(8,128)(2,1)} %win_ref.1) | copy-start | bytes 491524
  5.9 0.8 %copy-start.4 = (f32[64,64]{1,0:T(8,128)S(1)}, f32[64,64]{1,0:T(8,128)}, u32[]{:S(2)}) copy-start(f32[64,64]{1,0:T(8,128)} %iinv_ref.1) | copy-start | bytes 49156
  6.7 0.8 %copy-start.5 = (f32[64,64]{1,0:T(8,128)S(1)}, f32[64,64]{1,0:T(8,128)}, u32[]{:S(2)}) copy-start(f32[64,64]{1,0:T(8,128)} %oinv_ref.1) | copy-start | bytes 49156
  7.4 0.7 %copy-start.6 = (s32[2]{0:T(128)S(1)}, s32[2]{0:T(128)}, u32[]{:S(2)}) copy-start(s32[2]{0:T(128)} %tlen_ref.1) | copy-start | bytes 28

commit v2 on v0

v2 whole, which is shorter than its diff:
```python
import jax
import jax.numpy as jnp
from jax import lax
from jax.experimental import pallas as pl
from jax.experimental.pallas import tpu as pltpu
from jax.sharding import PartitionSpec as P

MESH = pl.DeviceIdType.MESH
F32 = jnp.float32
BF16 = jnp.bfloat16
HIGHEST = lax.Precision.HIGHEST
NT = (((1,), (1,)), ((), ()))

R = 64
QUARTER = 128
LEN = 512
HALF = 2048


def remote(src, dst, send_sem, recv_sem, device):
    return pltpu.make_async_remote_copy(
        src_ref=src,
        dst_ref=dst,
        send_sem=send_sem,
        recv_sem=recv_sem,
        device_id=device,
        device_id_type=MESH,
    )


def mod4(value):
    return lax.rem(value + 4, 4)


def kernel(
    tin_ref,
    tcot_ref,
    rin_ref,
    rcot_ref,
    tlen_ref,
    rlen,
    win_ref,
    wout_ref,
    iinv_ref,
    oinv_ref,
    store_ref,
    scores_ref,
    fresh_ref,
    tin,
    tcot,
    rin,
    rcot,
    win,
    wout,
    iinv,
    oinv,
    tlen,
    store,
    storep,
    po_send,
    po,
    pi_send,
    pi,
    mine,
    col,
    full,
    lhs,
    acc,
    accf,
    rpo,
    rscr,
    rpart_send,
    rpart_recv,
    trow,
    trowb,
    load_sem,
    po_ss,
    po_rs,
    pi_ss,
    pi_rs,
    col_ss,
    col_rs,
    s4_ss,
    s4_rs,
    s5_ss,
    s5_rs,
    fw_ss,
    fw_rs,
    rpo_ss,
    rpo_rs,
    rrs_ss,
    rrs_rs,
):
    me = lax.axis_index("store")
    t = lax.axis_index("tensor")
    c = lax.rem(me, 2)
    y = lax.rem(lax.div(me, 2), 4)
    zl = lax.rem(lax.div(me, 8), 2)
    x = lax.div(me, 16)

    def index(xx, zz, yy, cc):
        return ((xx * 2 + zz) * 4 + yy) * 2 + cc

    barrier = pltpu.get_barrier_semaphore()
    partners = [(me, mod4(t + 2)), (me, mod4(t + 1)), (me, mod4(t + 3))]
    for dt in (2, 1, 3, 0):
        for dz in range(2):
            for dc in range(2):
                if dz or dc:
                    partners.append(
                        (index(x, lax.rem(zl + dz, 2), y, lax.rem(c + dc, 2)), mod4(t + dt))
                    )
    for k in range(1, 4):
        partners.append((index(mod4(x + k), zl, y, c), t))
        partners.append((index(x, zl, mod4(y + k), c), t))

    load_wout = pltpu.make_async_copy(wout_ref, wout, load_sem.at[0])
    load_cot = [
        pltpu.make_async_copy(tcot_ref.at[n], tcot.at[n], load_sem.at[1 + n]) for n in range(2)
    ]
    load_oinv = pltpu.make_async_copy(oinv_ref, oinv, load_sem.at[3])
    load_iinv = pltpu.make_async_copy(iinv_ref, iinv, load_sem.at[4])
    load_win = pltpu.make_async_copy(win_ref, win, load_sem.at[5])
    load_in = [
        pltpu.make_async_copy(tin_ref.at[n], tin.at[n], load_sem.at[6 + n]) for n in range(2)
    ]
    load_tlen = pltpu.make_async_copy(tlen_ref, tlen, load_sem.at[8])
    load_rcot = pltpu.make_async_copy(rcot_ref.at[0], rcot, load_sem.at[10])
    load_rin = pltpu.make_async_copy(rin_ref.at[0], rin, load_sem.at[11])
    load_store = pltpu.make_async_copy(store_ref, store, load_sem.at[12])
    for partner in partners[:3]:
        pl.semaphore_signal(barrier, inc=1, device_id=partner, device_id_type=MESH)
    for copy in [load_wout, *load_cot, load_oinv, load_tlen, load_win, load_iinv, *load_in]:
        copy.start()
    for partner in partners[3:]:
        pl.semaphore_signal(barrier, inc=1, device_id=partner, device_id_type=MESH)

    lane = lax.broadcasted_iota(jnp.int32, (1, QUARTER), 1) + t * QUARTER

    def scale_of(length):
        lengths = jnp.full((1, QUARTER), length, jnp.int32)
        kept = jnp.where(lane < lengths, 1.0, 0.0).astype(F32)
        return kept / lengths.astype(F32)

    load_wout.wait()
    for copy in load_cot:
        copy.wait()
    pout = lax.dot_general(
        wout[...], tcot[...].reshape(2 * QUARTER, 5120), NT, preferred_element_type=F32
    )
    load_tlen.wait()
    scale = jnp.concatenate([scale_of(tlen[0]), scale_of(tlen[1])], axis=1)
    pout = pout * scale
    load_oinv.wait()
    left = jnp.concatenate([oinv[pl.ds(r, 16, stride=4), :] for r in range(4)], axis=0)
    pout = jnp.dot(left, pout, precision=HIGHEST, preferred_element_type=F32).astype(BF16)
    for n in range(2):
        po_send[n] = pout[:, n * QUARTER : (n + 1) * QUARTER]

    pl.semaphore_wait(barrier, len(partners))
    po_copies = []
    for k in (2, 1, 3):
        to = mod4(t + k)
        copy = remote(
            po_send.at[lax.div(to, 2)], po.at[t], po_ss.at[k - 1], po_rs.at[k - 1], (me, to)
        )
        copy.start()
        po_copies.append(copy)
    po[t] = po_send[lax.div(t, 2)]

    load_iinv.wait()
    load_win.wait()
    for copy in load_in:
        copy.wait()
    pin = lax.dot_general(
        win[...], tin[...].reshape(2 * LEN, 1280), NT, preferred_element_type=F32
    )
    pin = jnp.dot(iinv[...], pin, precision=HIGHEST, preferred_element_type=F32).astype(BF16)
    for u in range(4):
        n, d = u // 2, u % 2
        pi_send[u] = pin[d * 32 : d * 32 + 32, n * LEN : (n + 1) * LEN]
    pi_copies = []
    for k in (2, 1, 3):
        to = mod4(t + k)
        copy = remote(pi_send.at[to], pi.at[k - 1], pi_ss.at[k - 1], pi_rs.at[k - 1], (me, to))
        copy.start()
        pi_copies.append(copy)
    for copy in (load_rcot, load_rin, load_store):
        copy.start()

    load_rcot.wait()
    rout = lax.dot_general(wout[...], rcot[...], NT, preferred_element_type=F32)
    rout = rout * scale_of(rlen[0])
    rpo[t] = rout.astype(BF16)
    load_rin.wait()
    rpin = lax.dot_general(win[...], rin[...], NT, preferred_element_type=F32).astype(BF16)

    for k in (2, 1, 3):
        slot_in = mod4(t - k)
        remote(
            po.at[slot_in], po.at[slot_in], po_ss.at[k - 1], po_rs.at[k - 1], (me, slot_in)
        ).wait_recv()
    outs = jnp.concatenate([po[u] for u in range(4)], axis=1)
    part = lax.dot_general(outs, pi_send[t], NT, preferred_element_type=F32)
    for copy in pi_copies[1:] + pi_copies[:1]:
        copy.wait_recv()
    for k in range(3):
        part += lax.dot_general(outs, pi[k], NT, preferred_element_type=F32)
    mine[...] = jnp.concatenate([part[16 * r : 16 * r + 16] for r in range(4)], axis=1).astype(BF16)

    n = lax.div(t, 2)
    h = lax.rem(t, 2)
    slot = (zl * 2 + c) * 2 + n
    col_copies = []
    for dt, dz in ((2, 0), (2, 1), (1, 1), (3, 1), (1, 0), (3, 0), (0, 1)):
        i = dt * 2 + dz
        copy = remote(
            mine,
            col.at[slot],
            col_ss.at[i],
            col_rs.at[slot],
            (index(x, lax.rem(zl + dz, 2), y, h), mod4(t + dt)),
        )
        copy.start()
        col_copies.append(copy)
    own_copy = pltpu.make_async_copy(mine, col.at[slot], col_rs.at[slot])
    sib_copy = remote(mine, col.at[slot], col_ss.at[0], col_rs.at[slot], (index(x, zl, y, h), t))

    @pl.when(h == c)
    def _():
        own_copy.start()

    @pl.when(h != c)
    def _():
        sib_copy.start()

    rpo_copies = []
    for k in (2, 1, 3):
        copy = remote(
            rpo.at[t], rpo.at[t], rpo_ss.at[k - 1], rpo_rs.at[k - 1], (me, mod4(t + k))
        )
        copy.start()
        rpo_copies.append(copy)

    load_store.wait()
    from_lane = lax.broadcasted_iota(jnp.int32, (256, 256), 0)
    to_lane = lax.broadcasted_iota(jnp.int32, (256, 256), 1)
    target = (
        lax.rem(lax.div(from_lane, 32), 2) * 128
        + lax.div(from_lane, 64) * 32
        + lax.rem(from_lane, 32)
    )
    order = jnp.where(to_lane == target, 1.0, 0.0).astype(BF16)

    @pl.loop(0, 16)
    def _(g):
        moved = jnp.dot(
            store[:, pl.ds(pl.multiple_of(g * 256, 256), 256)], order, preferred_element_type=F32
        ).astype(BF16)
        at = pl.ds(pl.multiple_of(g * 128, 128), 128)
        storep[0, :, at] = moved[:, :128]
        storep[1, :, at] = moved[:, 128:]

    for i in range(8):
        pltpu.make_async_copy(mine, col.at[i], col_rs.at[i]).wait()

    for g in range(2):
        rows = jnp.swapaxes(col[:, 8 * g : 8 * g + 8, :].astype(F32), 0, 1)
        rows = rows.reshape(4, 16, 128).astype(BF16)
        full[c, x, y, 4 * g : 4 * g + 4] = rows

    first = x * (1 - c) + y * c
    second = y * (1 - c) + x * c
    sib = index(x, zl, y, 1 - c)

    def block(core, i, k, one, two):
        one, two = mod4(one - i), mod4(two - k)
        return full.at[core, one * (1 - core) + two * core, two * (1 - core) + one * core]

    s4_copies, s5_copies, fw_copies = [], [], []

    def send_first(k):
        to = index(mod4(x + k * (1 - c)), zl, mod4(y + k * c), c)
        ref = block(c, 0, 0, first, second)
        copy = remote(ref, ref, s4_ss.at[k - 1], s4_rs.at[k - 1], (to, t))
        copy.start()
        s4_copies.append(copy)

    def send_second(i, k):
        to = index(mod4(x + k * c), zl, mod4(y + k * (1 - c)), c)
        ref = block(c, i, 0, first, second)
        copy = remote(ref, ref, s5_ss.at[i, k - 1], s5_rs.at[i, k - 1], (to, t))
        copy.start()
        s5_copies.append(copy)

    def send_sibling(i, k):
        ref = block(c, i, k, first, second)
        copy = remote(ref, ref, fw_ss.at[i, k], fw_rs.at[i, k], (sib, t))
        copy.start()
        fw_copies.append(copy)

    def take(ref, send_sem, recv_sem):
        remote(ref, ref, send_sem, recv_sem, (sib, t)).wait_recv()

    for k in (2, 1, 3):
        send_first(k)
    for k in (2, 1, 3):
        send_second(0, k)
    send_sibling(0, 0)

    for k in (1, 3, 2):
        from_t = mod4(t - k)
        take(rpo.at[from_t], rpo_ss.at[k - 1], rpo_rs.at[k - 1])
    routs = jnp.concatenate([rpo[u] for u in range(4)], axis=1)
    rscr[...] = lax.dot_general(routs, rpin, NT, preferred_element_type=F32)
    for d in range(2):
        rpart_send[d] = jnp.concatenate(
            [rscr[pl.ds(r, 16, stride=4), :][:, 32 * d : 32 * d + 32] for r in range(4)], axis=1
        )
    rrs_copies = []
    for k in (2, 1, 3):
        copy = remote(
            rpart_send,
            rpart_recv.at[k - 1],
            rrs_ss.at[k - 1],
            rrs_rs.at[k - 1],
            (me, mod4(t + k)),
        )
        copy.start()
        rrs_copies.append(copy)

    for i in (1, 3, 2):
        take(block(c, i, 0, first, second), s4_ss.at[i - 1], s4_rs.at[i - 1])
        for k in (2, 1, 3):
            send_second(i, k)
        send_sibling(i, 0)
    for i in (0, 1, 3, 2):
        for k in (1, 3, 2):
            take(block(c, i, k, first, second), s5_ss.at[i, k - 1], s5_rs.at[i, k - 1])
            send_sibling(i, k)

    for copy in rrs_copies:
        copy.wait_recv()
    rtotal = rpart_send[...] + rpart_recv[0] + rpart_recv[1] + rpart_recv[2]
    trow[...] = jnp.zeros_like(trow)
    for d in range(2):
        for e in range(16):
            trow[d, 0:1, e * 128 : (e + 1) * 128] = rtotal[d, e : e + 1]
    trowb[...] = trow[...].astype(BF16)

    def gather_rows(core):
        for g in range(8):
            tiles = full[core, :, :, g].astype(F32).reshape(16, 2, 8, 128)
            for e in range(2):
                at = (2 * g + e) * 128
                lhs[:, at : at + 128] = tiles[:, e].reshape(128, 128).astype(BF16)

    gather_rows(c)
    acc[...] = lax.dot_general(lhs[...], storep[c], NT, preferred_element_type=F32)
    accf[:, 0:16] = lax.dot_general(lhs[...], trowb[c], NT, preferred_element_type=F32)
    for i in (0, 1, 3, 2):
        for k in (0, 1, 3, 2):
            take(block(1 - c, i, k, second, first), fw_ss.at[i, k], fw_rs.at[i, k])
    gather_rows(1 - c)
    acc[...] += lax.dot_general(lhs[...], storep[1 - c], NT, preferred_element_type=F32)
    accf[:, 0:16] += lax.dot_general(lhs[...], trowb[1 - c], NT, preferred_element_type=F32)

    columns = []
    for xx in range(4):
        for zz in range(2):
            for yp in range(2):
                row = xx * 32 + zz * 16 + yp * 8
                at = [(xx * 4 + yy) * 8 + zz * 4 for yy in (2 * yp, 2 * yp + 1)]
                scores_ref[row : row + 8, :] = jnp.concatenate(
                    [acc[i : i + 4, :] for i in at], axis=0
                )
                columns += [accf[i : i + 4, :] for i in at]
    fresh_ref[...] = jnp.swapaxes(jnp.concatenate(columns, axis=0), 0, 1)[0:1]

    for copy in (
        po_copies
        + pi_copies
        + col_copies
        + rpo_copies
        + s4_copies
        + rrs_copies
        + s5_copies
        + fw_copies
    ):
        copy.wait_send()

    @pl.when(h != c)
    def _():
        sib_copy.wait_send()


def body(*args):
    args = [
        arg if arg.shape == (1,) else pltpu.with_memory_space_constraint(arg, pltpu.HBM)
        for arg in args
    ]
    dma = pltpu.SemaphoreType.DMA
    hbm = pl.BlockSpec(memory_space=pltpu.HBM)
    vmem = pl.BlockSpec(memory_space=pltpu.VMEM)
    scores, fresh = pl.pallas_call(
        kernel,
        out_shape=(
            jax.ShapeDtypeStruct((128, 512), F32),
            jax.ShapeDtypeStruct((1, 128), F32),
        ),
        in_specs=[hbm] * 5 + [pl.BlockSpec(memory_space=pltpu.SMEM)] + [hbm] * 5,
        out_specs=(vmem, vmem),
        scratch_shapes=[
            pltpu.VMEM((2, LEN, 1280), BF16),
            pltpu.VMEM((2, QUARTER, 5120), BF16),
            pltpu.VMEM((LEN, 1280), BF16),
            pltpu.VMEM((QUARTER, 5120), BF16),
            pltpu.VMEM((R, 1280), BF16),
            pltpu.VMEM((R, 5120), BF16),
            pltpu.VMEM((R, R), F32),
            pltpu.VMEM((R, R), F32),
            pltpu.SMEM((2,), jnp.int32),
            pltpu.VMEM((512, 4096), BF16),
            pltpu.VMEM((2, 512, HALF), BF16),
            pltpu.VMEM((2, R, QUARTER), BF16),
            pltpu.VMEM((4, R, QUARTER), BF16),
            pltpu.VMEM((4, 32, LEN), BF16),
            pltpu.VMEM((3, 32, LEN), BF16),
            pltpu.VMEM((16, 128), BF16),
            pltpu.VMEM((8, 16, 128), BF16),
            pltpu.VMEM((2, 4, 4, 8, 16, 128), BF16),
            pltpu.VMEM((128, HALF), BF16),
            pltpu.VMEM((128, 512), F32),
            pltpu.VMEM((128, 128), F32),
            pltpu.VMEM((4, R, QUARTER), BF16),
            pltpu.VMEM((R, R), F32),
            pltpu.VMEM((2, 16, 128), F32),
            pltpu.VMEM((3, 2, 16, 128), F32),
            pltpu.VMEM((2, 16, HALF), F32),
            pltpu.VMEM((2, 16, HALF), BF16),
            dma((13,)),
            dma((3,)),
            dma((3,)),
            dma((3,)),
            dma((3,)),
            dma((8,)),
            dma((8,)),
            dma((3,)),
            dma((3,)),
            dma((4, 3)),
            dma((4, 3)),
            dma((4, 4)),
            dma((4, 4)),
            dma((3,)),
            dma((3,)),
            dma((3,)),
            dma((3,)),
        ],
        compiler_params=pltpu.CompilerParams(
            collective_id=0, has_side_effects=True, vmem_limit_bytes=40 * 1024 * 1024
        ),
    )(*args)
    return scores, fresh.reshape(128, 1)


def solution(mesh):
    return jax.shard_map(
        body,
        mesh=mesh,
        in_specs=(
            P("store", None, "tensor"),
            P("store", "tensor", None),
            P("store", None, "tensor"),
            P("store", "tensor", None),
            P("store"),
            P("store"),
            P(None, "tensor"),
            P(),
            P(),
            P(),
            P(("store", "tensor"), None),
        ),
        out_specs=(P(None, ("store", "tensor")), P(None, "store")),
        check_vma=False,
    )
```

time: 179 us -> 38.9 us (0.22)
  waiting for transfers between devices: 95.8 us -> 0 us
  blocking collectives: 46.4 us -> 0 us
  Pallas kernels: 0 us -> 36.3 us
  matrix products: 16.9 us -> 0 us
  between operations: 14.8 us -> 1.29 us
  local copies, waits for them, and re-layouts: 3.3 us -> 1.22 us
    all_gather x1 -> x0, waiting for transfers between devices: 95.8 us -> none  [body(): block_rows = lax.all_gather(conditioned, 'store', axis=0, tiled=True)]
    pallas_call x0 -> x1, Pallas kernels: none -> 36.3 us  [body(): pl.pallas_call(kernel, out_shape=(jax.ShapeDtypeStruct((128, 512), F32),...]
    all_gather x2 -> x0, blocking collectives: 24.8 us -> none  [the longest x1 14.1 us: body(): lax.all_gather(test_out, 'tensor', axis=2, tiled=True)]
    psum x1 -> x0, blocking collectives: 21.6 us -> none  [body(): full_test_in, full_train_in = lax.psum((test_in, train_in), 'tensor')]
    dot_general x10 -> x0, matrix products: 16.9 us -> none  [the longest x2 4.76 us: local_terms(): jnp.einsum('nld,rd->nrl', cotangents, out_projection, preferred_element_t...]
    unnamed x12 -> x2, local copies, waits for them, and re-layouts: 3.01 us -> 1.22 us
  transfers between devices with their start and end apart: 1 -> 0, of which waited for: 1 -> 0; matrix products, arithmetic and copies ran while one was open for 1% -> 0% of each run, Pallas kernels for 0% -> 0%
where the time goes in v2:
time: 38.9 us; the launch traced here: 38.8 us
  Pallas kernels  36.3 us (93%)
  between operations  1.29 us (3%)
  local copies, waits for them, and re-layouts  1.22 us (3%)
    pallas_call x1, Pallas kernels, body(): pl.pallas_call(kernel, out_shape=(jax.ShapeDtypeStruct((128, 512), F32),...  36.3 us
    unnamed x2, local copies, waits for them, and re-layouts  1.22 us

profile of v2, /device:TPU:1, one launch (start us, length us, event | category | flops | bytes accessed | tf_op | source)
XLA Modules:
  0.0 38.8 jit_solution(12088102702407348629)
XLA Ops:
  1.3 36.3 %shard_map.122 = (f32[128,512]{1,0:T(8,128)S(1)}, f32[1,128]{1,0:T(1,128)S(1)}) custom-call(bf16[2,512,1280]{2,1,0:T(8,128)(2,1)} %tin_ref.1, bf16[2,128,5120]{2,1,0:T(8,128)(2,1)} %tcot_ref.1, bf16[1,512,1280]{2,1,0:T(8,128)(2,1)} %rin_ref.1, bf16[1,128,5120]{2,1,0:T(8,128)(2,1)} %rcot_ref.1, s32[2]{0:T(128)} %tlen_ref.1, s32[1]{0:T(128)S(6)} %copy.15.rlen, ...), custom_call_target="tpu_custom_call" | custom-call | tf_op jit(solution)/shard_map/pallas_call | solution.py:405
  37.6 0.7 %copy.16 = f32[128,512]{1,0:T(8,128)} copy(f32[128,512]{1,0:T(8,128)S(1)} %get-tuple-element.8) | data formatting | bytes 524288
  38.3 0.5 %copy.17 = f32[128,1]{0,1:T(1,128)} copy(f32[128,1]{0,1:T(1,128)S(1)} %bitcast.1) | data formatting | bytes 1024

commit v3 on v2

v3 whole, which is shorter than its diff:
```python
import jax
import jax.numpy as jnp
from jax import lax
from jax.experimental import pallas as pl
from jax.experimental.pallas import tpu as pltpu
from jax.sharding import PartitionSpec as P

MESH = pl.DeviceIdType.MESH
F32 = jnp.float32
BF16 = jnp.bfloat16
NT = (((1,), (1,)), ((), ()))

R = 64
QUARTER = 128
LEN = 512
HALF = 2048


def remote(src, dst, send_sem, recv_sem, device):
    return pltpu.make_async_remote_copy(
        src_ref=src,
        dst_ref=dst,
        send_sem=send_sem,
        recv_sem=recv_sem,
        device_id=device,
        device_id_type=MESH,
    )


def split(value):
    high = value.astype(BF16)
    return high, (value - high.astype(F32)).astype(BF16)


def times(matrix, value):
    mh, ml = split(matrix)
    vh, vl = split(value)
    return jnp.dot(
        jnp.concatenate([mh, ml, mh, ml], axis=1),
        jnp.concatenate([vh, vh, vl, vl], axis=0),
        preferred_element_type=F32,
    )


def mod4(value):
    return lax.rem(value + 4, 4)


def kernel(
    tin_ref,
    tcot_ref,
    rin_ref,
    rcot_ref,
    tlen_ref,
    rlen,
    win_ref,
    wout_ref,
    iinv_ref,
    oinv_ref,
    store_ref,
    scores_ref,
    fresh_ref,
    tin,
    tcot,
    rin,
    rcot,
    win,
    wout,
    iinv,
    oinv,
    tlen,
    store,
    storep,
    pouts,
    pins,
    po_send,
    po,
    pi_send,
    pi,
    mine,
    full,
    rows,
    lhs,
    acc,
    accf,
    rpo,
    rscr,
    rpart_send,
    rpart_recv,
    trow,
    trowb,
    ready,
    load_sem,
    po_ss,
    po_rs,
    pi_ss,
    pi_rs,
    a_ss,
    a_rs,
    b_ss,
    b_rs,
    fw_ss,
    fw_rs,
    rpo_ss,
    rpo_rs,
    rrs_ss,
    rrs_rs,
):
    me = lax.axis_index("store")
    t = lax.axis_index("tensor")
    c = lax.rem(me, 2)
    y = lax.rem(lax.div(me, 2), 4)
    zl = lax.rem(lax.div(me, 8), 2)
    x = lax.div(me, 16)

    def index(xx, zz, yy, cc):
        return ((xx * 2 + zz) * 4 + yy) * 2 + cc

    n = lax.div(t, 2)
    h = lax.rem(t, 2)
    same = h == c
    first = x * (1 - c) + y * c
    second = y * (1 - c) + x * c
    sib = index(x, zl, y, 1 - c)

    load_wout = pltpu.make_async_copy(wout_ref, wout, load_sem.at[0])
    load_cot = pltpu.make_async_copy(tcot_ref, tcot, load_sem.at[1])
    load_oinv = pltpu.make_async_copy(oinv_ref, oinv, load_sem.at[4])
    load_iinv = pltpu.make_async_copy(iinv_ref, iinv, load_sem.at[5])
    load_win = pltpu.make_async_copy(win_ref, win, load_sem.at[6])
    load_in = pltpu.make_async_copy(tin_ref, tin, load_sem.at[7])
    load_tlen = pltpu.make_async_copy(tlen_ref, tlen, load_sem.at[8])
    load_rcot = pltpu.make_async_copy(rcot_ref.at[0], rcot, load_sem.at[9])
    load_rin = pltpu.make_async_copy(rin_ref.at[0], rin, load_sem.at[10])
    load_store = pltpu.make_async_copy(store_ref, store, load_sem.at[11])
    for copy in (load_wout, load_cot):
        copy.start()

    barrier = pltpu.get_barrier_semaphore()
    partners = []
    for dt in (2, 1, 3, 0):
        for dz in range(2):
            for dc in range(2):
                if dt or dz or dc:
                    partners.append(
                        (index(x, lax.rem(zl + dz, 2), y, lax.rem(c + dc, 2)), mod4(t + dt))
                    )
    for k in (2, 1, 3):
        partners.append((index(mod4(x + k), zl, y, c), t))
        partners.append((index(x, zl, mod4(y + k), c), t))
    for partner in partners:
        pl.semaphore_signal(barrier, inc=1, device_id=partner, device_id_type=MESH)
    for copy in (load_oinv, load_tlen, load_win, load_iinv, load_in):
        copy.start()

    lane = lax.broadcasted_iota(jnp.int32, (1, QUARTER), 1) + t * QUARTER

    def scale_of(length):
        lengths = jnp.full((1, QUARTER), length, jnp.int32)
        kept = jnp.where(lane < lengths, 1.0, 0.0).astype(F32)
        return kept / lengths.astype(F32)

    for copy in (load_wout, load_cot, load_win, load_in, load_tlen, load_oinv, load_iinv):
        copy.wait()
    pouts[...] = lax.dot_general(
        wout[...], tcot[...].reshape(2 * QUARTER, 5120), NT, preferred_element_type=F32
    )
    pins[...] = lax.dot_general(
        win[...], tin[...].reshape(2 * LEN, 1280), NT, preferred_element_type=F32
    )
    scale = jnp.concatenate([scale_of(tlen[0]), scale_of(tlen[1])], axis=1)
    left = jnp.concatenate([oinv[pl.ds(r, 16, stride=4), :] for r in range(4)], axis=0)
    pout = times(left, pouts[...] * scale).astype(BF16)
    for i in range(2):
        po_send[i] = pout[:, i * QUARTER : (i + 1) * QUARTER]
    pin = times(iinv[...], pins[...]).astype(BF16)
    for u in range(4):
        i, d = u // 2, u % 2
        pi_send[u] = pin[d * 32 : d * 32 + 32, i * LEN : (i + 1) * LEN]

    pl.semaphore_wait(barrier, len(partners))
    po_copies = []
    for k in (2, 1, 3):
        to = mod4(t + k)
        copy = remote(
            po_send.at[lax.div(to, 2)], po.at[t], po_ss.at[k - 1], po_rs.at[k - 1], (me, to)
        )
        copy.start()
        po_copies.append(copy)
    po[t] = po_send[n]

    pi_copies = []
    for k in (2, 1, 3):
        to = mod4(t + k)
        copy = remote(pi_send.at[to], pi.at[k - 1], pi_ss.at[k - 1], pi_rs.at[k - 1], (me, to))
        copy.start()
        pi_copies.append(copy)
    off = lax.rem(h + c, 2)
    for dt in (2, 0):
        for dz in range(2):
            for dc in range(2):
                whom = (
                    index(x, lax.rem(zl + dz, 2), y, lax.rem(c + dc, 2)),
                    mod4(t + off + dt),
                )
                if dt or dz or dc:
                    pl.semaphore_signal(ready, inc=1, device_id=whom, device_id_type=MESH)
                else:

                    @pl.when(jnp.logical_not(same))
                    def _():
                        pl.semaphore_signal(ready, inc=1, device_id=whom, device_id_type=MESH)

    for copy in (load_rcot, load_rin, load_store):
        copy.start()

    load_rcot.wait()
    rout = lax.dot_general(wout[...], rcot[...], NT, preferred_element_type=F32)
    rout = rout * scale_of(rlen[0])
    rpo[t] = rout.astype(BF16)
    load_rin.wait()
    rpin = lax.dot_general(win[...], rin[...], NT, preferred_element_type=F32).astype(BF16)

    for k in (2, 1, 3):
        slot_in = mod4(t - k)
        remote(
            po.at[slot_in], po.at[slot_in], po_ss.at[k - 1], po_rs.at[k - 1], (me, slot_in)
        ).wait_recv()
    outs = jnp.concatenate([po[u] for u in range(4)], axis=1)
    part = lax.dot_general(outs, pi_send[t], NT, preferred_element_type=F32)
    for copy in pi_copies[1:] + pi_copies[:1]:
        copy.wait_recv()
    for k in range(3):
        part += lax.dot_general(outs, pi[k], NT, preferred_element_type=F32)
    mine[...] = jnp.concatenate([part[16 * r : 16 * r + 16] for r in range(4)], axis=1).astype(BF16)

    pl.semaphore_wait(ready, 8 - same.astype(jnp.int32))
    slot = n * 4 + zl * 2 + c
    a_copies = []
    for k in (2, 1, 3, 0):
        for dt, dz in ((2, 0), (2, 1), (1, 1), (3, 1), (1, 0), (3, 0), (0, 1), (0, 0)):
            i = (k * 4 + dt) * 2 + dz
            to = index(mod4(x + k * (1 - h)), lax.rem(zl + dz, 2), mod4(y + k * h), h)
            copy = remote(
                mine, full.at[h, x, y, slot], a_ss.at[i], a_rs.at[k, slot], (to, mod4(t + dt))
            )
            if i:
                copy.start()
                a_copies.append(copy)
            else:
                sib_copy = copy
    own_copy = pltpu.make_async_copy(mine, full.at[h, x, y, slot], a_rs.at[0, slot])

    @pl.when(same)
    def _():
        own_copy.start()

    @pl.when(jnp.logical_not(same))
    def _():
        sib_copy.start()

    rpo_copies = []
    for k in (2, 1, 3):
        copy = remote(
            rpo.at[t], rpo.at[t], rpo_ss.at[k - 1], rpo_rs.at[k - 1], (me, mod4(t + k))
        )
        copy.start()
        rpo_copies.append(copy)

    load_store.wait()
    from_lane = lax.broadcasted_iota(jnp.int32, (256, 256), 1)
    to_lane = lax.broadcasted_iota(jnp.int32, (256, 256), 0)
    target = (
        lax.rem(lax.div(from_lane, 32), 2) * 128
        + lax.div(from_lane, 64) * 32
        + lax.rem(from_lane, 32)
    )
    order = jnp.where(to_lane == target, 1.0, 0.0).astype(BF16)

    @pl.loop(0, 16)
    def _(g):
        moved = lax.dot_general(
            order,
            store[:, pl.ds(pl.multiple_of(g * 256, 256), 256)],
            NT,
            preferred_element_type=F32,
        ).astype(BF16)
        at = pl.ds(pl.multiple_of(g * 128, 128), 128)
        storep[0, at, :] = moved[:128]
        storep[1, at, :] = moved[128:]

    def block(core, i, k, one, two, group):
        one, two = mod4(one - i), mod4(two - k)
        return full.at[
            core, one * (1 - core) + two * core, two * (1 - core) + one * core, pl.ds(group * 4, 4)
        ]

    b_copies, fw_copies = [], []

    def send_second(i, k, group):
        to = index(mod4(x + k * c), zl, mod4(y + k * (1 - c)), c)
        ref = block(c, i, 0, first, second, group)
        copy = remote(ref, ref, b_ss.at[i, group, k - 1], b_rs.at[i, group, k - 1], (to, t))
        copy.start()
        b_copies.append(copy)

    def send_sibling(i, k, group):
        ref = block(c, i, k, first, second, group)
        copy = remote(ref, ref, fw_ss.at[i, group, k], fw_rs.at[i, group, k], (sib, t))
        copy.start()
        fw_copies.append(copy)

    def take(ref, send_sem, recv_sem):
        remote(ref, ref, send_sem, recv_sem, (sib, t)).wait_recv()

    def take_first(i, group):
        for j in range(4):
            one = mod4(first - i)
            piece = full.at[c, one * (1 - c) + second * c, second * (1 - c) + one * c, group * 4 + j]
            pltpu.make_async_copy(mine, piece, a_rs.at[i, group * 4 + j]).wait()
        for k in (2, 1, 3):
            send_second(i, k, group)
        send_sibling(i, 0, group)

    near = lax.div(mod4(t - c), 2)
    groups = (near, 1 - near)
    for i in (0, 1, 3, 2):
        take_first(i, near)

    for i in (0, 1, 3, 2):
        take_first(i, 1 - near)

    for k in (1, 3, 2):
        from_t = mod4(t - k)
        take(rpo.at[from_t], rpo_ss.at[k - 1], rpo_rs.at[k - 1])
    routs = jnp.concatenate([rpo[u] for u in range(4)], axis=1)
    rscr[...] = lax.dot_general(routs, rpin, NT, preferred_element_type=F32)
    for d in range(2):
        rpart_send[d] = jnp.concatenate(
            [rscr[pl.ds(r, 16, stride=4), :][:, 32 * d : 32 * d + 32] for r in range(4)], axis=1
        )
    rrs_copies = []
    for k in (2, 1, 3):
        copy = remote(
            rpart_send,
            rpart_recv.at[k - 1],
            rrs_ss.at[k - 1],
            rrs_rs.at[k - 1],
            (me, mod4(t + k)),
        )
        copy.start()
        rrs_copies.append(copy)

    for group in groups:
        for i in (0, 1, 3, 2):
            for k in (1, 3, 2):
                take(
                    block(c, i, k, first, second, group),
                    b_ss.at[i, group, k - 1],
                    b_rs.at[i, group, k - 1],
                )
                send_sibling(i, k, group)

    for copy in rrs_copies:
        copy.wait_recv()
    rtotal = rpart_send[...] + rpart_recv[0] + rpart_recv[1] + rpart_recv[2]
    trow[...] = jnp.zeros_like(trow)
    for d in range(2):
        for e in range(16):
            trow[d, 0:1, e * 128 : (e + 1) * 128] = rtotal[d, e : e + 1]
    trowb[...] = trow[...].astype(BF16)

    def gather_rows(core):
        for xx in range(4):
            for yy in range(4):
                for q in range(8):
                    row = xx * 32 + (q // 2 % 2) * 16 + yy * 4 + q % 2 * 2 + q // 4
                    rows[row * 16 : row * 16 + 16, :] = full[core, xx, yy, q].astype(F32)
        for e in range(16):
            lhs[:, e * 128 : e * 128 + 128] = rows[pl.ds(e, 128, stride=16), :].astype(BF16)

    gather_rows(c)
    acc[...] = jnp.dot(lhs[...], storep[c], preferred_element_type=F32)
    accf[...] = lax.dot_general(trowb[c], lhs[...], NT, preferred_element_type=F32)
    for group in range(2):
        for i in (0, 1, 3, 2):
            for k in (0, 1, 3, 2):
                take(
                    block(1 - c, i, k, second, first, group),
                    fw_ss.at[i, group, k],
                    fw_rs.at[i, group, k],
                )
    gather_rows(1 - c)
    scores_ref[...] = acc[...] + jnp.dot(lhs[...], storep[1 - c], preferred_element_type=F32)
    total = accf[...] + lax.dot_general(trowb[1 - c], lhs[...], NT, preferred_element_type=F32)
    fresh_ref[...] = total[0:1]

    for copy in po_copies + pi_copies + a_copies + rpo_copies + rrs_copies + b_copies + fw_copies:
        copy.wait_send()

    @pl.when(jnp.logical_not(same))
    def _():
        sib_copy.wait_send()


def body(*args):
    args = [
        arg if arg.shape == (1,) else pltpu.with_memory_space_constraint(arg, pltpu.HBM)
        for arg in args
    ]
    dma = pltpu.SemaphoreType.DMA
    hbm = pl.BlockSpec(memory_space=pltpu.HBM)
    vmem = pl.BlockSpec(memory_space=pltpu.VMEM)
    scores, fresh = pl.pallas_call(
        kernel,
        out_shape=(
            jax.ShapeDtypeStruct((128, 512), F32),
            jax.ShapeDtypeStruct((1, 128), F32),
        ),
        in_specs=[hbm] * 5 + [pl.BlockSpec(memory_space=pltpu.SMEM)] + [hbm] * 5,
        out_specs=(vmem, vmem),
        scratch_shapes=[
            pltpu.VMEM((2, LEN, 1280), BF16),
            pltpu.VMEM((2, QUARTER, 5120), BF16),
            pltpu.VMEM((LEN, 1280), BF16),
            pltpu.VMEM((QUARTER, 5120), BF16),
            pltpu.VMEM((R, 1280), BF16),
            pltpu.VMEM((R, 5120), BF16),
            pltpu.VMEM((R, R), F32),
            pltpu.VMEM((R, R), F32),
            pltpu.SMEM((2,), jnp.int32),
            pltpu.VMEM((512, 4096), BF16),
            pltpu.VMEM((2, HALF, 512), BF16),
            pltpu.VMEM((R, 2 * QUARTER), F32),
            pltpu.VMEM((R, 2 * LEN), F32),
            pltpu.VMEM((2, R, QUARTER), BF16),
            pltpu.VMEM((4, R, QUARTER), BF16),
            pltpu.VMEM((4, 32, LEN), BF16),
            pltpu.VMEM((3, 32, LEN), BF16),
            pltpu.VMEM((16, 128), BF16),
            pltpu.VMEM((2, 4, 4, 8, 16, 128), BF16),
            pltpu.VMEM((128 * 16, 128), F32),
            pltpu.VMEM((128, HALF), BF16),
            pltpu.VMEM((128, 512), F32),
            pltpu.VMEM((16, 128), F32),
            pltpu.VMEM((4, R, QUARTER), BF16),
            pltpu.VMEM((R, R), F32),
            pltpu.VMEM((2, 16, 128), F32),
            pltpu.VMEM((3, 2, 16, 128), F32),
            pltpu.VMEM((2, 16, HALF), F32),
            pltpu.VMEM((2, 16, HALF), BF16),
            pltpu.SemaphoreType.REGULAR,
            dma((12,)),
            dma((3,)),
            dma((3,)),
            dma((3,)),
            dma((3,)),
            dma((32,)),
            dma((4, 8)),
            dma((4, 2, 3)),
            dma((4, 2, 3)),
            dma((4, 2, 4)),
            dma((4, 2, 4)),
            dma((3,)),
            dma((3,)),
            dma((3,)),
            dma((3,)),
        ],
        compiler_params=pltpu.CompilerParams(
            collective_id=0, has_side_effects=True, vmem_limit_bytes=40 * 1024 * 1024
        ),
    )(*args)
    return scores, fresh.reshape(128, 1)


def solution(mesh):
    return jax.shard_map(
        body,
        mesh=mesh,
        in_specs=(
            P("store", None, "tensor"),
            P("store", "tensor", None),
            P("store", None, "tensor"),
            P("store", "tensor", None),
            P("store"),
            P("store"),
            P(None, "tensor"),
            P(),
            P(),
            P(),
            P(("store", "tensor"), None),
        ),
        out_specs=(P(None, ("store", "tensor")), P(None, "store")),
        check_vma=False,
    )
```

time: 38.9 us -> 37.2 us (0.956)
  Pallas kernels: 36.3 us -> 34.6 us
    pallas_call x1, Pallas kernels: 36.3 us -> 34.6 us  [body(): pl.pallas_call(kernel, out_shape=(jax.ShapeDtypeStruct((128, 512), F32),...]
where the time goes in v3:
time: 37.2 us; the launch traced here: 37.1 us
  Pallas kernels  34.6 us (93%)
  between operations  1.29 us (3%)
  local copies, waits for them, and re-layouts  1.22 us (3%)
    pallas_call x1, Pallas kernels, body(): pl.pallas_call(kernel, out_shape=(jax.ShapeDtypeStruct((128, 512), F32),...  34.6 us
    unnamed x2, local copies, waits for them, and re-layouts  1.22 us

profile of v3, /device:TPU:1, one launch (start us, length us, event | category | flops | bytes accessed | tf_op | source)
XLA Modules:
  0.0 37.1 jit_solution(471366652993597776)
XLA Ops:
  1.3 34.6 %shard_map.122 = (f32[128,512]{1,0:T(8,128)S(1)}, f32[1,128]{1,0:T(1,128)S(1)}) custom-call(bf16[2,512,1280]{2,1,0:T(8,128)(2,1)} %tin_ref.1, bf16[2,128,5120]{2,1,0:T(8,128)(2,1)} %tcot_ref.1, bf16[1,512,1280]{2,1,0:T(8,128)(2,1)} %rin_ref.1, bf16[1,128,5120]{2,1,0:T(8,128)(2,1)} %rcot_ref.1, s32[2]{0:T(128)} %tlen_ref.1, s32[1]{0:T(128)S(6)} %copy.15.rlen, ...), custom_call_target="tpu_custom_call" | custom-call | tf_op jit(solution)/shard_map/pallas_call | solution.py:414
  35.9 0.7 %copy.16 = f32[128,512]{1,0:T(8,128)} copy(f32[128,512]{1,0:T(8,128)S(1)} %get-tuple-element.8) | data formatting | bytes 524288
  36.6 0.5 %copy.17 = f32[128,1]{0,1:T(1,128)} copy(f32[128,1]{0,1:T(1,128)S(1)} %bitcast.1) | data formatting | bytes 1024

commit v4 on v3

--- a/solution.py
+++ b/solution.py
@@ -40,6 +40,10 @@
         jnp.concatenate([vh, vh, vl, vl], axis=0),
         preferred_element_type=F32,
     )
+
+
+def take(ref, sem):
+    pltpu.make_async_copy(ref, ref, sem).wait()
 
 
 def mod4(value):
@@ -148,10 +152,10 @@
     for k in (2, 1, 3):
         partners.append((index(mod4(x + k), zl, y, c), t))
         partners.append((index(x, zl, mod4(y + k), c), t))
+    for copy in (load_oinv, load_tlen, load_win, load_iinv, load_in):
+        copy.start()
     for partner in partners:
         pl.semaphore_signal(barrier, inc=1, device_id=partner, device_id_type=MESH)
-    for copy in (load_oinv, load_tlen, load_win, load_iinv, load_in):
-        copy.start()
 
     lane = lax.broadcasted_iota(jnp.int32, (1, QUARTER), 1) + t * QUARTER
 
@@ -179,22 +183,18 @@
         pi_send[u] = pin[d * 32 : d * 32 + 32, i * LEN : (i + 1) * LEN]
 
     pl.semaphore_wait(barrier, len(partners))
-    po_copies = []
     for k in (2, 1, 3):
         to = mod4(t + k)
         copy = remote(
-            po_send.at[lax.div(to, 2)], po.at[t], po_ss.at[k - 1], po_rs.at[k - 1], (me, to)
+            po_send.at[lax.div(to, 2)], po.at[t], po_ss, po_rs, (me, to)
         )
         copy.start()
-        po_copies.append(copy)
     po[t] = po_send[n]
 
-    pi_copies = []
     for k in (2, 1, 3):
         to = mod4(t + k)
-        copy = remote(pi_send.at[to], pi.at[k - 1], pi_ss.at[k - 1], pi_rs.at[k - 1], (me, to))
-        copy.start()
-        pi_copies.append(copy)
+        copy = remote(pi_send.at[to], pi.at[k - 1], pi_ss, pi_rs, (me, to))
+        copy.start()
     off = lax.rem(h + c, 2)
     for dt in (2, 0):
         for dz in range(2):
@@ -221,35 +221,28 @@
     load_rin.wait()
     rpin = lax.dot_general(win[...], rin[...], NT, preferred_element_type=F32).astype(BF16)
 
-    for k in (2, 1, 3):
-        slot_in = mod4(t - k)
-        remote(
-            po.at[slot_in], po.at[slot_in], po_ss.at[k - 1], po_rs.at[k - 1], (me, slot_in)
-        ).wait_recv()
+    take(po.at[0:3], po_rs)
     outs = jnp.concatenate([po[u] for u in range(4)], axis=1)
     part = lax.dot_general(outs, pi_send[t], NT, preferred_element_type=F32)
-    for copy in pi_copies[1:] + pi_copies[:1]:
-        copy.wait_recv()
+    take(pi, pi_rs)
     for k in range(3):
         part += lax.dot_general(outs, pi[k], NT, preferred_element_type=F32)
     mine[...] = jnp.concatenate([part[16 * r : 16 * r + 16] for r in range(4)], axis=1).astype(BF16)
 
     pl.semaphore_wait(ready, 8 - same.astype(jnp.int32))
     slot = n * 4 + zl * 2 + c
-    a_copies = []
     for k in (2, 1, 3, 0):
         for dt, dz in ((2, 0), (2, 1), (1, 1), (3, 1), (1, 0), (3, 0), (0, 1), (0, 0)):
             i = (k * 4 + dt) * 2 + dz
             to = index(mod4(x + k * (1 - h)), lax.rem(zl + dz, 2), mod4(y + k * h), h)
             copy = remote(
-                mine, full.at[h, x, y, slot], a_ss.at[i], a_rs.at[k, slot], (to, mod4(t + dt))
+                mine, full.at[h, x, y, slot], a_ss.at[k if i else 4], a_rs.at[k, n], (to, mod4(t + dt))
             )
             if i:
                 copy.start()
-                a_copies.append(copy)
             else:
                 sib_copy = copy
-    own_copy = pltpu.make_async_copy(mine, full.at[h, x, y, slot], a_rs.at[0, slot])
+    own_copy = pltpu.make_async_copy(mine, full.at[h, x, y, slot], a_rs.at[0, n])
 
     @pl.when(same)
     def _():
@@ -259,13 +252,8 @@
     def _():
         sib_copy.start()
 
-    rpo_copies = []
     for k in (2, 1, 3):
-        copy = remote(
-            rpo.at[t], rpo.at[t], rpo_ss.at[k - 1], rpo_rs.at[k - 1], (me, mod4(t + k))
-        )
-        copy.start()
-        rpo_copies.append(copy)
+        remote(rpo.at[t], rpo.at[t], rpo_ss, rpo_rs, (me, mod4(t + k))).start()
 
     load_store.wait()
     from_lane = lax.broadcasted_iota(jnp.int32, (256, 256), 1)
@@ -295,29 +283,17 @@
             core, one * (1 - core) + two * core, two * (1 - core) + one * core, pl.ds(group * 4, 4)
         ]
 
-    b_copies, fw_copies = [], []
-
     def send_second(i, k, group):
         to = index(mod4(x + k * c), zl, mod4(y + k * (1 - c)), c)
         ref = block(c, i, 0, first, second, group)
-        copy = remote(ref, ref, b_ss.at[i, group, k - 1], b_rs.at[i, group, k - 1], (to, t))
-        copy.start()
-        b_copies.append(copy)
+        remote(ref, ref, b_ss, b_rs.at[i, group], (to, t)).start()
 
     def send_sibling(i, k, group):
         ref = block(c, i, k, first, second, group)
-        copy = remote(ref, ref, fw_ss.at[i, group, k], fw_rs.at[i, group, k], (sib, t))
-        copy.start()
-        fw_copies.append(copy)
-
-    def take(ref, send_sem, recv_sem):
-        remote(ref, ref, send_sem, recv_sem, (sib, t)).wait_recv()
+        remote(ref, ref, fw_ss, fw_rs, (sib, t)).start()
 
     def take_first(i, group):
-        for j in range(4):
-            one = mod4(first - i)
-            piece = full.at[c, one * (1 - c) + second * c, second * (1 - c) + one * c, group * 4 + j]
-            pltpu.make_async_copy(mine, piece, a_rs.at[i, group * 4 + j]).wait()
+        take(block(c, i, 0, first, second, group), a_rs.at[i, group])
         for k in (2, 1, 3):
             send_second(i, k, group)
         send_sibling(i, 0, group)
@@ -330,39 +306,30 @@
     for i in (0, 1, 3, 2):
         take_first(i, 1 - near)
 
-    for k in (1, 3, 2):
-        from_t = mod4(t - k)
-        take(rpo.at[from_t], rpo_ss.at[k - 1], rpo_rs.at[k - 1])
+    take(rpo.at[0:3], rpo_rs)
     routs = jnp.concatenate([rpo[u] for u in range(4)], axis=1)
     rscr[...] = lax.dot_general(routs, rpin, NT, preferred_element_type=F32)
     for d in range(2):
         rpart_send[d] = jnp.concatenate(
             [rscr[pl.ds(r, 16, stride=4), :][:, 32 * d : 32 * d + 32] for r in range(4)], axis=1
         )
-    rrs_copies = []
     for k in (2, 1, 3):
         copy = remote(
             rpart_send,
             rpart_recv.at[k - 1],
-            rrs_ss.at[k - 1],
-            rrs_rs.at[k - 1],
+            rrs_ss,
+            rrs_rs,
             (me, mod4(t + k)),
         )
         copy.start()
-        rrs_copies.append(copy)
 
     for group in groups:
         for i in (0, 1, 3, 2):
+            take(full.at[c, 0, 0:3, 0:4], b_rs.at[i, group])
             for k in (1, 3, 2):
-                take(
-                    block(c, i, k, first, second, group),
-                    b_ss.at[i, group, k - 1],
-                    b_rs.at[i, group, k - 1],
-                )
                 send_sibling(i, k, group)
 
-    for copy in rrs_copies:
-        copy.wait_recv()
+    take(rpart_recv, rrs_rs)
     rtotal = rpart_send[...] + rpart_recv[0] + rpart_recv[1] + rpart_recv[2]
     trow[...] = jnp.zeros_like(trow)
     for d in range(2):
@@ -382,21 +349,21 @@
     gather_rows(c)
     acc[...] = jnp.dot(lhs[...], storep[c], preferred_element_type=F32)
     accf[...] = lax.dot_general(trowb[c], lhs[...], NT, preferred_element_type=F32)
-    for group in range(2):
-        for i in (0, 1, 3, 2):
-            for k in (0, 1, 3, 2):
-                take(
-                    block(1 - c, i, k, second, first, group),
-                    fw_ss.at[i, group, k],
-                    fw_rs.at[i, group, k],
-                )
+    take(full.at[1 - c], fw_rs)
     gather_rows(1 - c)
     scores_ref[...] = acc[...] + jnp.dot(lhs[...], storep[1 - c], preferred_element_type=F32)
     total = accf[...] + lax.dot_general(trowb[1 - c], lhs[...], NT, preferred_element_type=F32)
     fresh_ref[...] = total[0:1]
 
-    for copy in po_copies + pi_copies + a_copies + rpo_copies + rrs_copies + b_copies + fw_copies:
-        copy.wait_send()
+    take(po.at[0:3], po_ss)
+    take(pi, pi_ss)
+    for k in range(1, 4):
+        take(full.at[0, 0, 0], a_ss.at[k])
+    take(full.at[0, 0, 0, 0:7], a_ss.at[0])
+    take(rpo.at[0:3], rpo_ss)
+    take(rpart_recv, rrs_ss)
+    take(full.at[0, 0:3], b_ss)
+    take(full.at[0], fw_ss)
 
     @pl.when(jnp.logical_not(same))
     def _():
@@ -451,20 +418,20 @@
             pltpu.VMEM((2, 16, HALF), BF16),
             pltpu.SemaphoreType.REGULAR,
             dma((12,)),
-            dma((3,)),
-            dma((3,)),
-            dma((3,)),
-            dma((3,)),
-            dma((32,)),
-            dma((4, 8)),
-            dma((4, 2, 3)),
-            dma((4, 2, 3)),
-            dma((4, 2, 4)),
-            dma((4, 2, 4)),
-            dma((3,)),
-            dma((3,)),
-            dma((3,)),
-            dma((3,)),
+            dma,
+            dma,
+            dma,
+            dma,
+            dma((5,)),
+            dma((4, 2)),
+            dma,
+            dma((4, 2)),
+            dma,
+            dma,
+            dma,
+            dma,
+            dma,
+            dma,
         ],
         compiler_params=pltpu.CompilerParams(
             collective_id=0, has_side_effects=True, vmem_limit_bytes=40 * 1024 * 1024

time: 37.2 us -> 35.6 us (0.957)
  Pallas kernels: 34.6 us -> 33.1 us
    pallas_call x1, Pallas kernels: 34.6 us -> 33.1 us  [body(): pl.pallas_call(kernel, out_shape=(jax.ShapeDtypeStruct((128, 512), F32),...]
where the time goes in v4:
time: 35.6 us
  Pallas kernels  33.1 us (93%)
  between operations  1.29 us (4%)
  local copies, waits for them, and re-layouts  1.22 us (3%)
    pallas_call x1, Pallas kernels, body(): pl.pallas_call(kernel, out_shape=(jax.ShapeDtypeStruct((128, 512), F32),...  33.1 us
    unnamed x2, local copies, waits for them, and re-layouts  1.22 us

profile of v4, /device:TPU:1, one launch (start us, length us, event | category | flops | bytes accessed | tf_op | source)
XLA Modules:
  0.0 35.6 jit_solution(15896302454635752943)
XLA Ops:
  1.3 33.1 %shard_map.122 = (f32[128,512]{1,0:T(8,128)S(1)}, f32[1,128]{1,0:T(1,128)S(1)}) custom-call(bf16[2,512,1280]{2,1,0:T(8,128)(2,1)} %tin_ref.1, bf16[2,128,5120]{2,1,0:T(8,128)(2,1)} %tcot_ref.1, bf16[1,512,1280]{2,1,0:T(8,128)(2,1)} %rin_ref.1, bf16[1,128,5120]{2,1,0:T(8,128)(2,1)} %rcot_ref.1, s32[2]{0:T(128)} %tlen_ref.1, s32[1]{0:T(128)S(6)} %copy.15.rlen, ...), custom_call_target="tpu_custom_call" | custom-call | tf_op jit(solution)/shard_map/pallas_call | solution.py:381
  34.3 0.7 %copy.16 = f32[128,512]{1,0:T(8,128)} copy(f32[128,512]{1,0:T(8,128)S(1)} %get-tuple-element.8) | data formatting | bytes 524288
  35.0 0.5 %copy.17 = f32[128,1]{0,1:T(1,128)} copy(f32[128,1]{0,1:T(1,128)S(1)} %bitcast.1) | data formatting | bytes 1024

commit v5 on v4

--- a/solution.py
+++ b/solution.py
@@ -128,16 +128,21 @@
     sib = index(x, zl, y, 1 - c)
 
     load_wout = pltpu.make_async_copy(wout_ref, wout, load_sem.at[0])
-    load_cot = pltpu.make_async_copy(tcot_ref, tcot, load_sem.at[1])
+    load_cot = [
+        pltpu.make_async_copy(tcot_ref.at[i], tcot.at[i], load_sem.at[1 + i]) for i in range(2)
+    ]
     load_oinv = pltpu.make_async_copy(oinv_ref, oinv, load_sem.at[4])
     load_iinv = pltpu.make_async_copy(iinv_ref, iinv, load_sem.at[5])
     load_win = pltpu.make_async_copy(win_ref, win, load_sem.at[6])
-    load_in = pltpu.make_async_copy(tin_ref, tin, load_sem.at[7])
+    load_in = [
+        pltpu.make_async_copy(tin_ref.at[i], tin.at[i], load_sem.at[pos])
+        for i, pos in enumerate((3, 7))
+    ]
     load_tlen = pltpu.make_async_copy(tlen_ref, tlen, load_sem.at[8])
     load_rcot = pltpu.make_async_copy(rcot_ref.at[0], rcot, load_sem.at[9])
     load_rin = pltpu.make_async_copy(rin_ref.at[0], rin, load_sem.at[10])
     load_store = pltpu.make_async_copy(store_ref, store, load_sem.at[11])
-    for copy in (load_wout, load_cot):
+    for copy in (load_wout, *load_cot):
         copy.start()
 
     barrier = pltpu.get_barrier_semaphore()
@@ -152,7 +157,7 @@
     for k in (2, 1, 3):
         partners.append((index(mod4(x + k), zl, y, c), t))
         partners.append((index(x, zl, mod4(y + k), c), t))
-    for copy in (load_oinv, load_tlen, load_win, load_iinv, load_in):
+    for copy in (load_oinv, load_tlen, load_win, load_iinv, *load_in):
         copy.start()
     for partner in partners:
         pl.semaphore_signal(barrier, inc=1, device_id=partner, device_id_type=MESH)
@@ -164,7 +169,7 @@
         kept = jnp.where(lane < lengths, 1.0, 0.0).astype(F32)
         return kept / lengths.astype(F32)
 
-    for copy in (load_wout, load_cot, load_win, load_in, load_tlen, load_oinv, load_iinv):
+    for copy in (load_wout, *load_cot, load_win, *load_in, load_tlen, load_oinv, load_iinv):
         copy.wait()
     pouts[...] = lax.dot_general(
         wout[...], tcot[...].reshape(2 * QUARTER, 5120), NT, preferred_element_type=F32
@@ -177,11 +182,6 @@
     pout = times(left, pouts[...] * scale).astype(BF16)
     for i in range(2):
         po_send[i] = pout[:, i * QUARTER : (i + 1) * QUARTER]
-    pin = times(iinv[...], pins[...]).astype(BF16)
-    for u in range(4):
-        i, d = u // 2, u % 2
-        pi_send[u] = pin[d * 32 : d * 32 + 32, i * LEN : (i + 1) * LEN]
-
     pl.semaphore_wait(barrier, len(partners))
     for k in (2, 1, 3):
         to = mod4(t + k)
@@ -190,6 +190,11 @@
         )
         copy.start()
     po[t] = po_send[n]
+
+    pin = times(iinv[...], pins[...]).astype(BF16)
+    for u in range(4):
+        i, d = u // 2, u % 2
+        pi_send[u] = pin[d * 32 : d * 32 + 32, i * LEN : (i + 1) * LEN]
 
     for k in (2, 1, 3):
         to = mod4(t + k)

time: 35.6 us -> 35.5 us (level)
  no operation moved by 1% of the time
where the time goes in v5:
time: 35.5 us; the launch traced here: 35.4 us
  Pallas kernels  32.9 us (93%)
  between operations  1.29 us (4%)
  local copies, waits for them, and re-layouts  1.22 us (3%)
    pallas_call x1, Pallas kernels, body(): pl.pallas_call(kernel, out_shape=(jax.ShapeDtypeStruct((128, 512), F32),...  32.9 us
    unnamed x2, local copies, waits for them, and re-layouts  1.22 us

profile of v5, /device:TPU:1, one launch (start us, length us, event | category | flops | bytes accessed | tf_op | source)
XLA Modules:
  0.0 35.4 jit_solution(994943306971872216)
XLA Ops:
  1.3 32.9 %shard_map.122 = (f32[128,512]{1,0:T(8,128)S(1)}, f32[1,128]{1,0:T(1,128)S(1)}) custom-call(bf16[2,512,1280]{2,1,0:T(8,128)(2,1)} %tin_ref.1, bf16[2,128,5120]{2,1,0:T(8,128)(2,1)} %tcot_ref.1, bf16[1,512,1280]{2,1,0:T(8,128)(2,1)} %rin_ref.1, bf16[1,128,5120]{2,1,0:T(8,128)(2,1)} %rcot_ref.1, s32[2]{0:T(128)} %tlen_ref.1, s32[1]{0:T(128)S(6)} %copy.15.rlen, ...), custom_call_target="tpu_custom_call" | custom-call | tf_op jit(solution)/shard_map/pallas_call | solution.py:386
  34.2 0.7 %copy.16 = f32[128,512]{1,0:T(8,128)} copy(f32[128,512]{1,0:T(8,128)S(1)} %get-tuple-element.8) | data formatting | bytes 524288
  34.9 0.5 %copy.17 = f32[128,1]{0,1:T(1,128)} copy(f32[128,1]{0,1:T(1,128)S(1)} %bitcast.1) | data formatting | bytes 1024

commit v6 on v5

--- a/solution.py
+++ b/solution.py
@@ -142,7 +142,7 @@
     load_rcot = pltpu.make_async_copy(rcot_ref.at[0], rcot, load_sem.at[9])
     load_rin = pltpu.make_async_copy(rin_ref.at[0], rin, load_sem.at[10])
     load_store = pltpu.make_async_copy(store_ref, store, load_sem.at[11])
-    for copy in (load_wout, *load_cot):
+    for copy in (load_oinv, load_tlen, load_iinv, load_wout, *load_cot, load_win, *load_in):
         copy.start()
 
     barrier = pltpu.get_barrier_semaphore()
@@ -157,8 +157,6 @@
     for k in (2, 1, 3):
         partners.append((index(mod4(x + k), zl, y, c), t))
         partners.append((index(x, zl, mod4(y + k), c), t))
-    for copy in (load_oinv, load_tlen, load_win, load_iinv, *load_in):
-        copy.start()
     for partner in partners:
         pl.semaphore_signal(barrier, inc=1, device_id=partner, device_id_type=MESH)
 
@@ -169,7 +167,11 @@
         kept = jnp.where(lane < lengths, 1.0, 0.0).astype(F32)
         return kept / lengths.astype(F32)
 
-    for copy in (load_wout, *load_cot, load_win, *load_in, load_tlen, load_oinv, load_iinv):
+    for copy in (load_oinv, load_tlen, load_iinv):
+        copy.wait()
+    left = jnp.concatenate([oinv[pl.ds(r, 16, stride=4), :] for r in range(4)], axis=0)
+    scale = jnp.concatenate([scale_of(tlen[0]), scale_of(tlen[1])], axis=1)
+    for copy in (load_wout, *load_cot, load_win, *load_in):
         copy.wait()
     pouts[...] = lax.dot_general(
         wout[...], tcot[...].reshape(2 * QUARTER, 5120), NT, preferred_element_type=F32
@@ -177,8 +179,6 @@
     pins[...] = lax.dot_general(
         win[...], tin[...].reshape(2 * LEN, 1280), NT, preferred_element_type=F32
     )
-    scale = jnp.concatenate([scale_of(tlen[0]), scale_of(tlen[1])], axis=1)
-    left = jnp.concatenate([oinv[pl.ds(r, 16, stride=4), :] for r in range(4)], axis=0)
     pout = times(left, pouts[...] * scale).astype(BF16)
     for i in range(2):
         po_send[i] = pout[:, i * QUARTER : (i + 1) * QUARTER]

time: 35.5 us -> 35.5 us (level)
  no operation moved by 1% of the time
where the time goes in v6:
time: 35.5 us; the launch traced here: 35.4 us
  Pallas kernels  32.9 us (93%)
  between operations  1.29 us (4%)
  local copies, waits for them, and re-layouts  1.22 us (3%)
    pallas_call x1, Pallas kernels, body(): pl.pallas_call(kernel, out_shape=(jax.ShapeDtypeStruct((128, 512), F32),...  32.9 us
    unnamed x2, local copies, waits for them, and re-layouts  1.22 us

profile of v6, /device:TPU:1, one launch (start us, length us, event | category | flops | bytes accessed | tf_op | source)
XLA Modules:
  0.0 35.4 jit_solution(12459289438079678473)
XLA Ops:
  1.3 32.9 %shard_map.122 = (f32[128,512]{1,0:T(8,128)S(1)}, f32[1,128]{1,0:T(1,128)S(1)}) custom-call(bf16[2,512,1280]{2,1,0:T(8,128)(2,1)} %tin_ref.1, bf16[2,128,5120]{2,1,0:T(8,128)(2,1)} %tcot_ref.1, bf16[1,512,1280]{2,1,0:T(8,128)(2,1)} %rin_ref.1, bf16[1,128,5120]{2,1,0:T(8,128)(2,1)} %rcot_ref.1, s32[2]{0:T(128)} %tlen_ref.1, s32[1]{0:T(128)S(6)} %copy.15.rlen, ...), custom_call_target="tpu_custom_call" | custom-call | tf_op jit(solution)/shard_map/pallas_call | solution.py:386
  34.2 0.7 %copy.16 = f32[128,512]{1,0:T(8,128)} copy(f32[128,512]{1,0:T(8,128)S(1)} %get-tuple-element.8) | data formatting | bytes 524288
  34.9 0.5 %copy.17 = f32[128,1]{0,1:T(1,128)} copy(f32[128,1]{0,1:T(1,128)S(1)} %bitcast.1) | data formatting | bytes 1024
